TPU v7x, 32 devices: a whole 2x2x4 slice. The times are simulated.
32 devices in a mesh: band: 4 (over y, core), fft: 8 (over z, x).
Axes of the slice: x: 2, y: 2, z: 4, core: 2. Of those that a mesh axis runs over, the one named last changes fastest.
Arguments:
- wave_coeffs: bfloat16 [4, 2, 192, 192, 256], P('band', None, None, 'fft'), may hold values from -4 to 4
- occupation: float32 [4, 2], P('band'), may hold values from 0.05 to 0.2
- potential: bfloat16 [192, 192, 256], P('fft'), may hold values from -1.5 to 1.5
- projectors: bfloat16 [32, 8, 64, 128], P('fft'), may hold values from -0.0625 to 0.0625
- coupling: float32 [8, 8], replicated, may hold values from -4 to 4
- sphere_blocks: int32 [32, 64], replicated, may hold values from 0 to 73727, as said below
Outputs:
- applied: bfloat16 [4, 2, 192, 192, 256], P('band', None, None, 'fft')
- rho: bfloat16 [192, 192, 256], P('fft')
- projections: float32 [4, 32, 2, 8], P('band', 'fft')
Inputs may be any that keep to these rules, and one draw needn't show every extreme that they name: `sphere_blocks`: row a holds 64 distinct block numbers. The first-dimension planes of all of them lie among the planes b * 24 - 6 to b * 24 + 29, counted around the periodic grid, with b = a // 4; every row has 16 blocks in the lowest of these planes and 16 in the highest.
All inputs are finite; a program needn't handle non-finite values.
Results may differ from a plain program's by a relative error of at most 0.025.
Values may be sent and summed in bfloat16 or wider, within the bound.
No kernel may reach another device: no remote copies, remote signals or barrier semaphores. Data moves between devices by JAX's collectives and lax.ppermute only.
A program may use at most 128 MiB of HBM per device.

v0:
```python
import functools
import math

import jax
import jax.numpy as jnp
import numpy as np
from jax import lax
from jax.experimental import pallas as pl
from jax.experimental.pallas import tpu as pltpu
from jax.sharding import PartitionSpec as P

HALO = 6
EDGE = 8
PLANES = 4
COLUMNS = 8
FOUR = 4
VMEM_BYTES = 56 * 1024 * 1024


def extended(shard, sides, width):
    for axis, dim in sides:
        count, length = (lax.axis_size(axis), shard.shape[dim])
        up = [(i, (i + 1) % count) for i in range(count)]
        down = [(j, i) for i, j in up]
        last = lax.slice_in_dim(shard, length - width, length, axis=dim)
        first = lax.slice_in_dim(shard, 0, width, axis=dim)
        before = lax.ppermute(last, axis, up)
        after = lax.ppermute(first, axis, down)
        shard = jnp.concatenate([before, shard, after], axis=dim)
    return shard


def dft_table(length, sign_value):
    indices = jnp.arange(length, dtype=jnp.int32)
    phases = indices[:, None] * indices[None, :] % length
    angles = 2.0 * math.pi / length * phases.astype(jnp.float32)
    factor = 1.0 / math.sqrt(length)
    cosine = jnp.cos(angles) * factor
    sine_part = jnp.sin(angles) * (sign_value * factor)
    upper_rows = jnp.stack([cosine, -sine_part])
    bottom = jnp.stack([sine_part, cosine])
    return jnp.stack([upper_rows, bottom]).astype(jnp.bfloat16)


def wave_squares(indices, length):
    frequency = (
        jnp.where(2 * indices < length, indices, indices - length).astype(jnp.float32) / length
    )
    return frequency * frequency


def per_device_plain(wave_coeffs, occupation, potential, projectors, coupling, sphere_blocks):
    pieces = lax.axis_size("fft")
    slab_index = lax.axis_index("fft")
    coeffs = wave_coeffs[0]
    size_x = coeffs.shape[1]
    columns = coeffs.shape[2]
    size_z = coeffs.shape[3]
    slab_planes = potential.shape[0]
    size_y = potential.shape[1]
    atom_dev = projectors.shape[0]
    nproj_count = projectors.shape[1]
    block_cells = projectors.shape[3]
    zblocks = size_z // block_cells
    plane_blocks = size_y * zblocks
    total_atoms = atom_dev * pieces
    table_x = dft_table(size_x, 1.0).transpose(0, 2, 1, 3).reshape(2 * size_x, 2 * size_x)
    inverse_y = dft_table(size_y, 1.0)
    inverse_z = dft_table(size_z, 1.0)
    flattened = coeffs.reshape(2 * size_x, columns * size_z)
    along_x = jnp.dot(table_x, flattened, preferred_element_type=jnp.float32)
    along_x = along_x.reshape(2, size_x, columns, size_z).astype(jnp.bfloat16)
    along_y = jnp.einsum(
        "abyk,bxkz->axyz",
        inverse_y,
        lax.all_to_all(along_x, "fft", split_axis=1, concat_axis=2, tiled=True),
        preferred_element_type=jnp.float32,
    ).astype(jnp.bfloat16)
    wave_field = jnp.einsum(
        "abzk,bxyk->axyz", inverse_z, along_y, preferred_element_type=jnp.float32
    ).astype(jnp.bfloat16)
    weights = occupation[0]
    real_part = wave_field[0].astype(jnp.float32)
    imag_part = wave_field[1].astype(jnp.float32)
    partial_density = weights[0] * real_part * real_part + weights[1] * imag_part * imag_part
    density = lax.psum(partial_density.astype(jnp.bfloat16), "band")
    strength = 3.0 * math.sqrt(block_cells * projectors.shape[2]) / nproj_count
    coupled = (coupling + coupling.T) * (0.5 * strength)
    nearby = extended(projectors, (("fft", 0),), atom_dev)
    atom_rows = (
        slab_index * atom_dev - atom_dev + jnp.arange(3 * atom_dev, dtype=jnp.int32) + total_atoms
    ) % total_atoms
    near_blocks = sphere_blocks[atom_rows]
    plane_index = near_blocks // plane_blocks
    inside = plane_index // slab_planes == slab_index
    local_index = jnp.where(
        inside,
        (plane_index - slab_index * slab_planes) * plane_blocks + near_blocks % plane_blocks,
        0,
    )
    blocks_own = wave_field.reshape(2, slab_planes * plane_blocks, block_cells)
    gathered = blocks_own[:, local_index] * inside[None, :, :, None].astype(jnp.bfloat16)
    partial_value = jnp.einsum(
        "ajsk,bask->abj", nearby, gathered, preferred_element_type=jnp.float32
    )
    summed = extended(partial_value, (("fft", 0),), atom_dev)
    projections_own = (
        summed[:atom_dev] + summed[2 * atom_dev : 3 * atom_dev] + summed[4 * atom_dev :]
    )
    energy_own = jnp.einsum(
        "ij,abj->abi", coupled, projections_own, precision=lax.Precision.HIGHEST
    )
    energy = extended(energy_own, (("fft", 0),), atom_dev)
    spread = jnp.einsum(
        "ajsk,abj->bask", nearby.astype(jnp.float32), energy, precision=lax.Precision.HIGHEST
    )
    spread = spread * inside[None, :, :, None].astype(jnp.float32)
    accumulated = (
        jnp.zeros((2, slab_planes * plane_blocks, block_cells), jnp.float32)
        .at[:, local_index]
        .add(spread)
    )
    nonlocal_term = accumulated.reshape(2, slab_planes, size_y, size_z)
    total_field = (
        potential.astype(jnp.float32)[None] * wave_field.astype(jnp.float32) + nonlocal_term
    ).astype(jnp.bfloat16)
    forward_z = dft_table(size_z, -1.0)
    forward_y = dft_table(size_y, -1.0)
    forward_x = dft_table(size_x, -1.0)
    back_z = jnp.einsum(
        "abzk,bxyk->axyz", forward_z, total_field, preferred_element_type=jnp.float32
    ).astype(jnp.bfloat16)
    back_y = jnp.einsum(
        "abyk,bxkz->axyz", forward_y, back_z, preferred_element_type=jnp.float32
    ).astype(jnp.bfloat16)
    transformed = jnp.einsum(
        "abxk,bkyz->axyz",
        forward_x,
        lax.all_to_all(back_y, "fft", split_axis=2, concat_axis=1, tiled=True),
        preferred_element_type=jnp.float32,
    )
    index_x = jnp.arange(size_x, dtype=jnp.int32)
    index_y = slab_index * columns + jnp.arange(columns, dtype=jnp.int32)
    index_z = jnp.arange(size_z, dtype=jnp.int32)
    kinetic = (
        wave_squares(index_x, size_x)[:, None, None]
        + wave_squares(index_y, size_y)[None, :, None]
        + wave_squares(index_z, size_z)[None, None, :]
    )
    applied = (transformed + kinetic[None] * coeffs.astype(jnp.float32)).astype(jnp.bfloat16)
    return (applied[None], density, projections_own[None])


def real_blocks(length, sign):
    index = np.arange(length)
    angles = 2.0 * np.pi / length * (index[:, None] * index[None, :] % length)
    cosine = np.cos(angles) / np.sqrt(length)
    sine = sign * np.sin(angles) / np.sqrt(length)
    blocks = np.empty((2, length, 2, length))
    blocks[0, :, 0, :] = cosine
    blocks[1, :, 1, :] = cosine
    blocks[0, :, 1, :] = -sine
    blocks[1, :, 0, :] = sine
    return blocks


def chunk_planes(slab_planes):
    low, high = list(range(EDGE)), list(range(slab_planes - EDGE, slab_planes))
    return [low + high, list(range(EDGE, slab_planes - EDGE))]


def params(steps):
    return pltpu.CompilerParams(
        dimension_semantics=("arbitrary",) * steps, vmem_limit_bytes=VMEM_BYTES
    )


def cost(products, values):
    return pl.CostEstimate(flops=4 * products, bytes_accessed=4 * values, transcendentals=0)


def whole(shape):
    return pl.BlockSpec(shape, lambda i: (0,) * len(shape))


SMEM_SPEC = pl.BlockSpec(memory_space=pltpu.SMEM)


def paired(refs, slab):
    return [(lax.bitwise_xor(slab, jnp.int32(k)), ref) for k, ref in enumerate(refs)]


def ring_order(pieces):
    return [0] + sorted(range(1, pieces), key=lambda k: abs(k - pieces // 2))


def shifted(refs, slab):
    order = ring_order(len(refs))
    return [(lax.rem(slab + k, len(refs)), ref) for k, ref in zip(order, refs)]


def first_x_kernel(slab, table_ref, coeffs_ref, *refs, pieces, natural):
    scratch = 3 if natural else 2
    outs = paired(refs[:-scratch], slab[0])
    turned, wide, *tall = refs[-scratch:]
    parts, size_x, columns, lanes = coeffs_ref.shape
    rows = parts * size_x
    height = table_ref.shape[0] // pieces

    for k, (device, _) in enumerate(outs):
        start = pl.multiple_of(device * height, 16)
        turned[k * height : (k + 1) * height, :] = table_ref[pl.ds(start, height), :]

    pitch = columns + 1

    def widen(k, carry):
        for part in range(parts):
            wide[pl.ds((part * size_x + k) * pitch, columns), :] = coeffs_ref[part, k].astype(
                jnp.float32
            )
        return carry

    lax.fori_loop(0, size_x, widen, 0, unroll=8)

    def some_columns(g, carry):
        loaded = [
            wide[pl.ds(COLUMNS * g + h, rows, stride=pitch), :].astype(jnp.bfloat16)
            for h in range(COLUMNS)
        ]
        for first in range(0, COLUMNS, FOUR):
            result = jnp.dot(
                turned[...],
                jnp.concatenate(loaded[first : first + FOUR], axis=1),
                preferred_element_type=jnp.float32,
            )
            for h in range(FOUR):
                column = COLUMNS * g + first + h
                piece = result[:, h * lanes : (h + 1) * lanes]
                if natural:
                    place = (first + h) % 2 * columns + COLUMNS // 2 * g + (first + h) // 2
                    planes = height // 2
                    for k in range(pieces):
                        for part in range(2):
                            start = k * height * columns + part * (columns // 2) + place
                            row = k * height + part * planes
                            tall[0][pl.ds(start, planes, stride=2 * columns), :] = piece[
                                row : row + planes
                            ]
                else:
                    piece = piece.astype(jnp.bfloat16)
                    for k, (_, out) in enumerate(outs):
                        out[column] = piece[k * height : (k + 1) * height]
        return carry

    lax.fori_loop(0, columns // COLUMNS, some_columns, 0)
    if natural:
        for k, (_, out) in enumerate(outs):
            values = tall[0][k * height * columns : (k + 1) * height * columns, :]
            out[...] = values.astype(jnp.bfloat16).reshape(out.shape)


def first_x(slab, table, coeffs, planes, pieces, natural):
    _, size_x, columns, size_z = coeffs.shape
    lanes = size_z // 2
    shape = (planes, 2 * columns) if natural else (columns, 2 * planes)
    scratch = [
        pltpu.VMEM(table.shape, jnp.bfloat16),
        pltpu.VMEM((2 * size_x * (columns + 1), lanes), jnp.float32),
    ]
    if natural:
        scratch.append(pltpu.VMEM((2 * pieces * planes * columns, lanes), jnp.float32))
    out_specs = [pl.BlockSpec((*shape, lanes), lambda i: (0, 0, i))] * pieces
    out_shape = [jax.ShapeDtypeStruct((*shape, size_z), jnp.bfloat16)] * pieces
    return pl.pallas_call(
        functools.partial(first_x_kernel, pieces=pieces, natural=natural),
        grid=(2,),
        in_specs=[
            SMEM_SPEC,
            whole(table.shape),
            pl.BlockSpec((2, size_x, columns, lanes), lambda i: (0, 0, 0, i)),
        ],
        out_specs=out_specs,
        out_shape=out_shape,
        scratch_shapes=scratch,
        compiler_params=params(1),
        cost_estimate=cost(2 * size_x * pieces * planes * columns * size_z, 2 * size_x * columns * size_z),
        name="first_x",
    )(slab, table, coeffs)


def ones_at(codes, count, axis):
    shape = (codes.shape[0], count) if axis == 1 else (count, codes.shape[1])
    places = lax.broadcasted_iota(jnp.int32, shape, axis)
    return jnp.where(codes == places, 1.0, 0.0).astype(jnp.bfloat16)


def field_kernel(slab, weights, table_y, table_z, codes, sides, *refs, pieces, count, natural):
    bufs = paired(refs[:count], slab[0])
    wave, density, *rows_out, gathered, wide = refs[count:]
    _, near, size_y, size_z = wave.shape
    columns = size_y // pieces
    groups, entries, _ = codes.shape
    lanes = 128
    halves = size_z // lanes
    i, last = pl.program_id(0), pl.num_programs(0) - 1
    planes = near * (last + 1)

    @pl.when(i == 0)
    def _():
        gathered[...] = jnp.zeros_like(gathered)

    loaded = []
    if natural:
        for source, buf in bufs:
            wide[source] = buf[...]
        for h in range(near):
            loaded.append(
                [wide[:, h, s * columns : (s + 1) * columns].reshape(size_y, size_z) for s in (0, 1)]
            )
    else:
        rows = bufs[0][1].shape[1]
        pitch = rows + 1

        @pl.when(i == 0)
        def _():
            for source, buf in bufs:

                def widen(column, carry):
                    values = buf[column].astype(jnp.float32)
                    for q in range(halves):
                        wide[q, pl.ds((source * columns + column) * pitch, rows), :] = values[
                            :, q * lanes : (q + 1) * lanes
                        ]
                    return carry

                lax.fori_loop(0, columns, widen, 0, unroll=8)

        def strided(start):
            return jnp.concatenate(
                [
                    wide[q, pl.ds(start, size_y // 2, stride=2 * pitch), :]
                    for q in range(halves)
                ],
                axis=1,
            ).astype(jnp.bfloat16)

        for h in range(near):
            plane = i * near + h
            loaded.append(
                [
                    jnp.concatenate(
                        [strided(s * pitch + part * planes + plane) for part in range(2)], axis=0
                    )
                    for s in (0, 1)
                ]
            )
    even, odd = (
        jnp.dot(
            table_y[s],
            jnp.concatenate([pair[s] for pair in loaded], axis=1),
            preferred_element_type=jnp.float32,
        )
        for s in (0, 1)
    )
    low, high = (even + odd).astype(jnp.bfloat16), (even - odd).astype(jnp.bfloat16)
    middle = size_y // 2
    turned = []
    for h in range(near):
        span = slice(h * size_z, (h + 1) * size_z)
        both = [
            jnp.concatenate(
                [values[part * middle : (part + 1) * middle, span] for values in (low, high)], axis=0
            )
            for part in range(2)
        ]
        turned.append(jnp.concatenate(both, axis=1))
    result = jnp.dot(
        jnp.concatenate(turned, axis=0), table_z[...], preferred_element_type=jnp.float32
    ).astype(jnp.bfloat16)
    for h in range(near):
        total = jnp.zeros((size_y, size_z), jnp.float32)
        for part in range(2):
            values = result[h * size_y : (h + 1) * size_y, part * size_z : (part + 1) * size_z]
            wave[part, h] = values
            values = values.astype(jnp.float32)
            total += weights[0, part] * values * values
        density[h] = total.astype(jnp.bfloat16)

    used = [0] if groups == 1 else [0, 1 + (2 * i > last).astype(jnp.int32)]
    for group in used:
        places = ones_at(codes[group] - i * near * size_y, near * size_y, 1)
        gathered[group] += jnp.dot(places, result, preferred_element_type=jnp.float32)

    @pl.when(i == last)
    def _():
        for group in range(groups):
            for part in range(2):
                total = jnp.zeros((entries, lanes), jnp.float32)
                for q in range(halves):
                    start = part * size_z + q * lanes
                    total += jnp.where(
                        sides[group] == q, gathered[group, :, start : start + lanes], 0.0
                    )
                rows_out[group][part] = total.astype(jnp.bfloat16)


def make_field(slab, weights, bufs, table_y, table_z, codes, sides, planes, pieces, natural):
    size_z = bufs[0].shape[-1]
    size_y = table_y.shape[1]
    columns = size_y // pieces
    groups, entries, _ = codes.shape
    if natural:
        buf_spec = pl.BlockSpec((PLANES, 2 * columns, size_z), lambda i: (i, 0, 0))
        wide = pltpu.VMEM((pieces, PLANES, 2 * columns, size_z), jnp.bfloat16)
    else:
        buf_spec = whole(bufs[0].shape)
        wide = pltpu.VMEM((size_z // 128, (2 * planes + 1) * size_y, 128), jnp.float32)
    return pl.pallas_call(
        functools.partial(field_kernel, pieces=pieces, count=len(bufs), natural=natural),
        grid=(planes // PLANES,),
        in_specs=[SMEM_SPEC, SMEM_SPEC]
        + [whole(a.shape) for a in (table_y, table_z, codes, sides)]
        + [buf_spec] * len(bufs),
        out_specs=[
            pl.BlockSpec((2, PLANES, size_y, size_z), lambda i: (0, i, 0, 0)),
            pl.BlockSpec((PLANES, size_y, size_z), lambda i: (i, 0, 0)),
        ]
        + [whole((2, entries, 128))] * groups,
        out_shape=[
            jax.ShapeDtypeStruct((2, planes, size_y, size_z), jnp.bfloat16),
            jax.ShapeDtypeStruct((planes, size_y, size_z), jnp.bfloat16),
        ]
        + [jax.ShapeDtypeStruct((2, entries, 128), jnp.bfloat16)] * groups,
        scratch_shapes=[pltpu.VMEM((groups, entries, 2 * size_z), jnp.float32), wide],
        compiler_params=params(1),
        cost_estimate=cost(
            2 * planes * size_y * size_z * (size_y + size_z), 2 * planes * size_y * size_z
        ),
        name="make_field",
    )(slab, weights, table_y, table_z, codes, sides, *bufs)


def nonlocal_kernel(coupled, projectors, *refs):
    parts, (projections, spread) = refs[:-2], refs[-2:]
    atoms, nproj, blocks, cells = projectors.shape
    for atom in range(atoms):
        tables = [projectors[atom, j].astype(jnp.float32) for j in range(nproj)]
        place = pl.ds(atom * blocks, blocks)
        for part in range(2):
            rows = sum(p[part, place].astype(jnp.float32) for p in parts)
            tile = jnp.concatenate(
                [jnp.sum(t * rows, axis=0, keepdims=True) for t in tables], axis=0
            )
            mixed = jnp.zeros_like(tile)
            for j in range(nproj):
                mixed += coupled[j] * tile[j : j + 1]
            projections[atom, part] = jnp.broadcast_to(
                jnp.sum(tile, -1, keepdims=True), tile.shape
            )
            energy = jnp.broadcast_to(jnp.sum(mixed, -1, keepdims=True), tile.shape)
            spread[part, place] = sum(
                t * energy[j : j + 1] for j, t in enumerate(tables)
            ).astype(jnp.bfloat16)


def make_nonlocal(coupled, projectors, parts):
    atoms, nproj, _, cells = projectors.shape
    return pl.pallas_call(
        nonlocal_kernel,
        out_shape=[
            jax.ShapeDtypeStruct((atoms, 2, nproj, cells), jnp.float32),
            jax.ShapeDtypeStruct(parts[0].shape, jnp.bfloat16),
        ],
        name="make_nonlocal",
    )(coupled, projectors, *parts)


def back_kernel(slab, wave, potential, table_z, table_y, codes, sides, *refs, pieces, natural):
    groups, _, entries = codes.shape
    sources, outs = refs[:groups], refs[groups:-2]
    spread, tall = refs[-2:]
    outs = shifted(outs, slab[0])
    near, size_y, size_z = potential.shape
    lanes = 128
    halves = size_z // lanes
    i, last = pl.program_id(0), pl.num_programs(0) - 1
    planes = near * (last + 1)

    @pl.when(i == 0)
    def _():
        for group, source in enumerate(sources):
            for part in range(2):
                for q in range(halves):
                    start = part * size_z + q * lanes
                    spread[group, :, start : start + lanes] = jnp.where(
                        sides[group] == q, source[part].astype(jnp.float32), 0.0
                    ).astype(jnp.bfloat16)

    used = [0] if groups == 1 else [0, 1 + (2 * i > last).astype(jnp.int32)]
    extra = jnp.zeros((near * size_y, 2 * size_z), jnp.float32)
    for group in used:
        places = ones_at(codes[group] - i * near * size_y, near * size_y, 0)
        extra += jnp.dot(places, spread[group], preferred_element_type=jnp.float32)
    fields = []
    for h in range(near):
        local = potential[h].astype(jnp.float32)
        both = [
            local * wave[part, h].astype(jnp.float32)
            + extra[h * size_y : (h + 1) * size_y, part * size_z : (part + 1) * size_z]
            for part in range(2)
        ]
        fields.append(jnp.concatenate(both, axis=1).astype(jnp.bfloat16))
    back_z = jnp.dot(
        jnp.concatenate(fields, axis=0), table_z[...], preferred_element_type=jnp.float32
    )
    middle = size_y // 2
    folded = [[], []]
    for h in range(near):
        low = back_z[h * size_y : h * size_y + middle]
        high = back_z[h * size_y + middle : (h + 1) * size_y]
        for kept, values in zip(folded, (low + high, low - high)):
            values = values.astype(jnp.bfloat16)
            kept.append(jnp.concatenate([values[:, :size_z], values[:, size_z:]], axis=0))
    columns = size_y // pieces
    for s, kept in enumerate(folded):
        back_y = jnp.dot(
            table_y[s], jnp.concatenate(kept, axis=1), preferred_element_type=jnp.float32
        )
        if natural:
            back_y = back_y.astype(jnp.bfloat16)
            for h in range(near):
                tall[:, h, s * columns : (s + 1) * columns] = back_y[
                    :, h * size_z : (h + 1) * size_z
                ].reshape(pieces, columns, size_z)
            continue
        pitch = outs[0][1].shape[1] + 1
        for h in range(near):
            for part in range(2):
                for q in range(halves):
                    start = s * pitch + part * planes + i * near + h
                    lane = h * size_z + q * lanes
                    tall[q, pl.ds(start, middle, stride=2 * pitch), :] = back_y[
                        part * middle : (part + 1) * middle, lane : lane + lanes
                    ]

    if natural:
        for target, out in outs:
            out[...] = tall[target]
        return
    rows = outs[0][1].shape[1]

    @pl.when(i == last)
    def _():
        for target, out in outs:

            def narrow(column, carry):
                start = (target * columns + column) * pitch
                values = [tall[q, pl.ds(start, rows), :] for q in range(halves)]
                out[column] = jnp.concatenate(values, axis=1).astype(jnp.bfloat16)
                return carry

            lax.fori_loop(0, columns, narrow, 0, unroll=8)


def go_back(slab, wave, potential, table_z, table_y, codes, sides, sources, place, pieces, natural):
    _, planes, size_y, size_z = wave.shape
    columns = size_y // pieces
    groups, _, entries = codes.shape
    scratch = [pltpu.VMEM((groups, entries, 2 * size_z), jnp.bfloat16)]
    if natural:
        shape = (planes, 2 * columns, size_z)
        out_specs = [pl.BlockSpec((PLANES, 2 * columns, size_z), lambda i: (i, 0, 0))] * pieces
        scratch.append(pltpu.VMEM((pieces, PLANES, 2 * columns, size_z), jnp.bfloat16))
    else:
        shape = (columns, 2 * planes, size_z)
        out_specs = [whole(shape)] * pieces
        scratch.append(pltpu.VMEM((size_z // 128, (2 * planes + 1) * size_y, 128), jnp.float32))
    return pl.pallas_call(
        functools.partial(back_kernel, pieces=pieces, natural=natural),
        grid=(planes // PLANES,),
        in_specs=[
            SMEM_SPEC,
            pl.BlockSpec((2, PLANES, size_y, size_z), lambda i: (0, i, 0, 0)),
            pl.BlockSpec((PLANES, size_y, size_z), lambda i: (place(i), 0, 0)),
        ]
        + [whole(a.shape) for a in (table_z, table_y, codes, sides, *sources)],
        out_specs=out_specs,
        out_shape=[jax.ShapeDtypeStruct(shape, jnp.bfloat16)] * pieces,
        scratch_shapes=scratch,
        compiler_params=params(1),
        cost_estimate=cost(
            2 * planes * size_y * size_z * (size_y + size_z), 2 * planes * size_y * size_z
        ),
        name="go_back",
    )(slab, wave, potential, table_z, table_y, codes, sides, *sources)


def last_x_kernel(frequency_x, frequency_yz, table, coeffs, *refs):
    bufs, (out, tall) = refs[:-2], refs[-2:]
    parts, size_x, columns, lanes = coeffs.shape
    pitch = columns + 1

    def some_columns(g, carry):
        loaded = []
        for h in range(COLUMNS):
            loaded.append(jnp.concatenate([buf[COLUMNS * g + h] for buf in bufs], axis=0))
        for first in range(0, COLUMNS, FOUR):
            result = jnp.dot(
                table[...],
                jnp.concatenate(loaded[first : first + FOUR], axis=1),
                preferred_element_type=jnp.float32,
            )
            for h in range(FOUR):
                tall[pl.ds(COLUMNS * g + first + h, parts * size_x, stride=pitch), :] = result[
                    :, h * lanes : (h + 1) * lanes
                ]
        return carry

    lax.fori_loop(0, columns // COLUMNS, some_columns, 0)

    def finish(k, carry):
        kinetic = frequency_x[k] + frequency_yz[...]
        for part in range(parts):
            out[part, k] = (
                tall[pl.ds((part * size_x + k) * pitch, columns), :] + kinetic * coeffs[part, k].astype(jnp.float32)
            ).astype(jnp.bfloat16)
        return carry

    lax.fori_loop(0, size_x, finish, 0, unroll=8)


def last_x(frequency_x, frequency_yz, table, coeffs, bufs):
    _, size_x, columns, size_z = coeffs.shape
    lanes = size_z // 2
    spec = pl.BlockSpec((2, size_x, columns, lanes), lambda i: (0, 0, 0, i))
    return pl.pallas_call(
        last_x_kernel,
        grid=(2,),
        in_specs=[
            SMEM_SPEC,
            pl.BlockSpec((columns, lanes), lambda i: (0, i)),
            whole(table.shape),
            spec,
        ]
        + [pl.BlockSpec((*b.shape[:2], lanes), lambda i: (0, 0, i)) for b in bufs],
        out_specs=spec,
        out_shape=jax.ShapeDtypeStruct(coeffs.shape, jnp.bfloat16),
        scratch_shapes=[pltpu.VMEM((2 * size_x * (columns + 1), lanes), jnp.float32)],
        compiler_params=params(1),
        cost_estimate=cost(2 * size_x * size_x * columns * size_z, 3 * size_x * columns * size_z),
        name="last_x",
    )(frequency_x, frequency_yz, table, coeffs, *bufs)


def per_device_chunked(wave_coeffs, occupation, potential, projectors, coupling, sphere_blocks):
    pieces = lax.axis_size("fft")
    bands = lax.axis_size("band")
    slab = lax.axis_index("fft")
    coeffs = wave_coeffs[0]
    _, size_x, columns, size_z = coeffs.shape
    slab_planes, size_y, _ = potential.shape
    atom_dev, nproj, blocks, cells = projectors.shape
    zblocks = size_z // cells
    outer, inner = chunk_planes(slab_planes)
    up = [(i, (i + 1) % pieces) for i in range(pieces)]
    down = [(j, i) for i, j in up]

    order = ring_order(pieces)
    inverse_x, forward_x = (real_blocks(size_x, s) for s in (1.0, -1.0))
    inverse_y, forward_y = (real_blocks(size_y, s) for s in (1.0, -1.0))
    inverse_z, forward_z = (real_blocks(size_z, s) for s in (1.0, -1.0))
    place_outer, place_inner = (
        np.arange(pieces)[:, None] * slab_planes + np.array(chunk)[None, :]
        for chunk in (outer, inner)
    )
    table_x_outer = np.stack([inverse_x[r][place_outer] for r in range(2)], 1)
    table_x_inner = np.stack([inverse_x[r][place_inner] for r in range(2)], 1)
    tables_back_x = [
        np.stack([forward_x[:, :, r][:, :, place] for r in range(2)], 3).reshape(
            2 * size_x, pieces, -1
        )
        for place in (place_outer, place_inner)
    ]
    middle = size_y // 2
    down_y = [inverse_y[:, :middle, :, s::2] for s in (0, 1)]
    back_y = [forward_y[:, s::2, :, :middle] for s in (0, 1)]
    split = (pieces, columns // 2)
    tables = [
        table_x_outer.reshape(-1, 2 * size_x),
        table_x_inner.reshape(-1, 2 * size_x),
        np.stack([t.reshape(size_y, -1) for t in down_y]),
        np.stack(
            [t.reshape(2, middle, 2, *split).swapaxes(2, 3).reshape(size_y, -1) for t in down_y]
        ),
        inverse_z.transpose(2, 3, 0, 1).reshape(2 * size_z, -1),
        forward_z.transpose(2, 3, 0, 1).reshape(2 * size_z, -1),
        np.stack([t.reshape(size_y, -1) for t in back_y]),
        np.stack([t.reshape(2, *split, -1).swapaxes(0, 1).reshape(size_y, -1) for t in back_y]),
        np.stack(
            [
                np.concatenate(
                    [t[:, (d - np.array(order)) % pieces].reshape(2 * size_x, -1) for t in tables_back_x],
                    axis=1,
                )
                for d in range(pieces)
            ]
        ),
    ]
    (
        table_x_outer, table_x_inner, table_y_outer, table_y_inner, table_z,
        table_back_z, table_back_y_outer, table_back_y_inner, tables_back_x,
    ) = (jnp.asarray(t.astype(jnp.bfloat16)) for t in tables)

    table_back_x = lax.dynamic_index_in_dim(tables_back_x, slab, 0, keepdims=False)

    where = slab.reshape(1)
    section_outer = first_x(where, table_x_outer, coeffs, len(outer), pieces, False)
    section_outer, table_x_inner, sphere_blocks = lax.optimization_barrier(
        (section_outer, table_x_inner, sphere_blocks)
    )
    section_inner = first_x(where, table_x_inner, coeffs, len(inner), pieces, True)

    entries = atom_dev * blocks

    def codes_of(chunk, shift):
        owner = (slab + shift + pieces) % pieces
        numbers = lax.dynamic_slice_in_dim(sphere_blocks, owner * atom_dev, atom_dev, 0)
        plane = numbers // (size_y * zblocks) - slab * slab_planes
        rest = numbers % (size_y * zblocks)
        if chunk is outer:
            inside = ((plane >= 0) & (plane < EDGE)) | (
                (plane >= slab_planes - EDGE) & (plane < slab_planes)
            )
            plane = jnp.where(plane < EDGE, plane, plane - len(inner))
        else:
            inside = (plane >= EDGE) & (plane < slab_planes - EDGE)
            plane = plane - EDGE
        code = jnp.where(inside, plane * size_y + rest // zblocks, -1)
        return code.reshape(entries), (rest % zblocks).reshape(entries)

    found = [codes_of(outer, shift) for shift in (0, -1, 1)]
    codes_outer, sides_outer = (jnp.stack(values) for values in zip(*found))
    codes_inner, sides_inner = (values[None] for values in codes_of(inner, 0))
    sides_outer, sides_inner = sides_outer[:, :, None], sides_inner[:, :, None]
    rows_codes = [codes_outer[:, :, None], codes_inner[:, :, None]]
    lane_codes = [codes_outer[:, None, :], codes_inner[:, None, :]]
    strength = 3.0 * math.sqrt(cells * blocks) / nproj
    coupled = (coupling + coupling.T) * (0.5 * strength)
    coupled = jnp.broadcast_to(coupled.T[:, :, None], (nproj, nproj, cells))
    section_inner, rows_codes, lane_codes, sides_outer, sides_inner, coupled = (
        lax.optimization_barrier(
            (section_inner, rows_codes, lane_codes, sides_outer, sides_inner, coupled)
        )
    )

    half = pieces // 2
    near, far = list(range(1, half)), list(range(half, pieces))

    def send(block, k, *awaited):
        for row, m in awaited:
            block, row[m] = lax.optimization_barrier((block, row[m]))
        return lax.ppermute(block, "fft", [(j, j ^ k) for j in range(pieces)])

    received_outer, received_inner = (
        [section[0]] + [None] * (pieces - 1) for section in (section_outer, section_inner)
    )
    for partners in (near, far):
        queue = [(section_outer, received_outer, k) for k in partners]
        queue += [(section_inner, received_inner, k) for k in partners]
        for place, (section, received, k) in enumerate(queue):
            awaited = [queue[place - 2][1:]] if place >= 2 else []
            received[k] = send(section[k], k, *awaited)
    wave_outer, density_outer, rows_outer, to_previous, to_following = make_field(
        where, occupation, received_outer, table_y_outer, table_z, rows_codes[0],
        sides_outer, len(outer), pieces, False,
    )
    from_following = lax.ppermute(to_previous, "fft", down)
    from_previous = lax.ppermute(to_following, "fft", up)
    density_outer = lax.psum(density_outer, "band")
    wave_inner, density_inner, rows_inner = make_field(
        where, occupation, received_inner, table_y_inner, table_z, rows_codes[1],
        sides_inner, len(inner), pieces, True,
    )
    projected, spread = make_nonlocal(
        coupled, projectors, [rows_outer, rows_inner, from_following, from_previous]
    )
    spread_previous = lax.ppermute(spread, "fft", up)
    spread_following = lax.ppermute(spread, "fft", down)
    edge_steps = EDGE // PLANES
    inner_steps = len(inner) // PLANES
    back_inner = go_back(
        where, wave_inner, potential, table_back_z, table_back_y_inner, lane_codes[1],
        sides_inner, [spread], lambda i: i + edge_steps, pieces, True,
    )
    def permute_all(values):
        received = [values[0]]
        for k, block in zip(order[1:], values[1:]):
            pairs = [(j, (j + k) % pieces) for j in range(pieces)]
            received.append(lax.ppermute(block, "fft", pairs))
        return received

    back_inner = permute_all(back_inner)
    back_outer = go_back(
        where, wave_outer, potential, table_back_z, table_back_y_outer, lane_codes[0],
        sides_outer, [spread, spread_previous, spread_following],
        lambda i: jnp.where(i < edge_steps, i, i + inner_steps), pieces, False,
    )
    density_inner, density_outer = lax.optimization_barrier((density_inner, density_outer))
    density_inner = lax.psum(density_inner, "band")
    back_outer, density_outer = lax.optimization_barrier((back_outer, density_outer))
    back_outer = permute_all(back_outer)
    back_inner = [
        b.reshape(len(inner), 2, 2, columns // 2, size_z)
        .transpose(3, 1, 2, 0, 4)
        .reshape(columns, -1, size_z)
        for b in back_inner
    ]
    density = jnp.concatenate([density_outer[:EDGE], density_inner, density_outer[EDGE:]], axis=0)

    index_x = np.arange(size_x)
    frequency_x = jnp.asarray(
        (np.where(2 * index_x < size_x, index_x, index_x - size_x) / size_x) ** 2, jnp.float32
    )
    index_y = slab * columns + jnp.arange(columns, dtype=jnp.int32)
    index_z = jnp.arange(size_z, dtype=jnp.int32)
    frequency_yz = wave_squares(index_y, size_y)[:, None] + wave_squares(index_z, size_z)[None, :]
    coeffs, density, back_inner = lax.optimization_barrier((coeffs, density, back_inner))
    applied = last_x(frequency_x, frequency_yz, table_back_x, coeffs, back_outer + back_inner)
    return (applied[None], density, projected[None, :, :, :, 0])


def per_device(wave_coeffs, occupation, potential, projectors, coupling, sphere_blocks):
    pieces, bands = lax.axis_size("fft"), lax.axis_size("band")
    size_z = wave_coeffs.shape[4]
    columns = wave_coeffs.shape[3]
    slab_planes = potential.shape[0]
    chunked = (
        pieces >= 4
        and pieces & (pieces - 1) == 0
        and slab_planes % EDGE == 0
        and slab_planes >= 3 * EDGE
        and EDGE >= HALO
        and columns % 8 == 0
        and size_z % 256 == 0
        and projectors.shape[0] % bands == 0
        and projectors.shape[3] == 128
        and projectors.shape[1] == 8
    )
    chosen = per_device_chunked if chunked else per_device_plain
    return chosen(wave_coeffs, occupation, potential, projectors, coupling, sphere_blocks)


def solution(mesh):
    placed = (
        P("band", None, None, "fft", None),
        P("band", None),
        P("fft", None, None),
        P("fft", None, None, None),
        P(),
        P(),
    )
    return jax.shard_map(
        per_device,
        mesh=mesh,
        in_specs=placed,
        out_specs=(
            P("band", None, None, "fft", None),
            P("fft", None, None),
            P("band", "fft", None, None),
        ),
        check_vma=False,
    )
```

profile of v0, /device:TPU:10, one launch (start us, length us, event | category | flops | bytes accessed | tf_op | source)
XLA Modules:
  0.0 275.4 jit_solution(5495494964577832875)
XLA Ops:
  7.2 6.4 %first_x.2 = (bf16[24,32,256]{2,1,0:T(8,128)(2,1)}, bf16[24,32,256]{2,1,0:T(8,128)(2,1)}, bf16[24,32,256]{2,1,0:T(8,128)(2,1)}, bf16[24,32,256]{2,1,0:T(8,128)(2...) custom-call(s32[1]{0:T(128)} %bitcast.2.slab, ...), custom_call_target="tpu_custom_call" | custom-call | flops 1207959552 | bytes 9437184 | tf_op jit(solution)/shard_map/first_x/pallas_call | solution.py:274
  18.6 6.1 %collective-permute-done.refs_1_ = bf16[24,32,256]{2,1,0:T(8,128)(2,1)S(1)} collective-permute-done((bf16[24,32,256]{2,1,0:T(8,128)(2,1)}, bf16[24,32,256]{2,1,0:T(8,128)(2,1)S(1)}, u32[]{:S(2)}, u32[]{:S(2)}) %collective-permute-start) | collective-permute-done | bytes 393248 | tf_op jit(solution)/shard_map/ppermute | solution.py:762
  24.8 17.2 %collective-permute-done.3.refs_4_ = bf16[24,32,256]{2,1,0:T(8,128)(2,1)S(1)} collective-permute-done((bf16[24,32,256]{2,1,0:T(8,128)(2,1)}, bf16[24,32,256]{2,1,0:T(8,128)(2,1)S(1)}, u32[]{:S(2)}, u32[]{:S(2)}) %collective-permute-start.3) | collective-permute-done | bytes 393248 | tf_op jit(solution)/shard_map/ppermute | solution.py:762
  42.4 9.2 %collective-permute-done.4.refs_5_ = bf16[24,32,256]{2,1,0:T(8,128)(2,1)S(1)} collective-permute-done((bf16[24,32,256]{2,1,0:T(8,128)(2,1)}, bf16[24,32,256]{2,1,0:T(8,128)(2,1)S(1)}, u32[]{:S(2)}, u32[]{:S(2)}) %collective-permute-start.4) | collective-permute-done | bytes 393248 | tf_op jit(solution)/shard_map/ppermute | solution.py:762
  54.9 5.7 %first_x.3 = (bf16[8,48,256]{2,1,0:T(8,128)(2,1)}, bf16[8,48,256]{2,1,0:T(8,128)(2,1)}, bf16[8,48,256]{2,1,0:T(8,128)(2,1)}, bf16[8,48,256]{2,1,0:T(8,128)(2,1)}...) custom-call(s32[1]{0:T(128)} %bitcast.2.slab, ...), custom_call_target="tpu_custom_call" | custom-call | flops 603979776 | bytes 9437184 | tf_op jit(solution)/shard_map/first_x/pallas_call | solution.py:274
  63.6 12.9 %collective-permute-done.5.refs_6_ = bf16[24,32,256]{2,1,0:T(8,128)(2,1)S(1)} collective-permute-done((bf16[24,32,256]{2,1,0:T(8,128)(2,1)}, bf16[24,32,256]{2,1,0:T(8,128)(2,1)S(1)}, u32[]{:S(2)}, u32[]{:S(2)}) %collective-permute-start.5) | collective-permute-done | bytes 393248 | tf_op jit(solution)/shard_map/ppermute | solution.py:762
  76.5 8.3 %collective-permute-done.6.refs_7_ = bf16[24,32,256]{2,1,0:T(8,128)(2,1)S(1)} collective-permute-done((bf16[24,32,256]{2,1,0:T(8,128)(2,1)}, bf16[24,32,256]{2,1,0:T(8,128)(2,1)S(1)}, u32[]{:S(2)}, u32[]{:S(2)}) %collective-permute-start.6) | collective-permute-done | bytes 393248 | tf_op jit(solution)/shard_map/ppermute | solution.py:762
  84.8 3.1 %collective-permute-start.10 = (bf16[8,48,256]{2,1,0:T(8,128)(2,1)}, bf16[8,48,256]{2,1,0:T(8,128)(2,1)S(1)}, u32[]{:S(2)}, u32[]{:S(2)}) collective-permute-start(bf16[8,48,256]{2,1,0:T(8,128)(2,1)} %get-tuple-element.166), channel_id=1, source_target_pairs={{0,4},{1,5},{2,6},{3,7},{4,0},{5,1},{6,2},{7,3},{8,12},{9,13},{10,... | collective-permute-start | bytes 589832 | tf_op jit(solution)/shard_map/ppermute | solution.py:762
  87.9 10.1 %make_field.2 = (bf16[2,16,192,256]{3,2,1,0:T(8,128)(2,1)}, bf16[16,192,256]{2,1,0:T(8,128)(2,1)}, bf16[2,256,128]{2,1,0:T(8,128)(2,1)}, bf16[2,256,128]{2,1,0:T(8,128)(2,1)}, bf16[2,256,128]{2,1,0:T(8,128)(2,1)}) custom-call(s32[1]{0:T(128)} %bitcast.2.slab, f32[1,2]{1,0:T(1,128)} %weights.3, bf16[2,192,192]{2,1,0:T(8,128)(2,1)} %constant.176.clone.table_y, ...), custom_call_target="tpu_custom_call" | custom-call | flops 2818572288 | bytes 6291456 | tf_op jit(solution)/shard_map/make_field/pallas_call | solution.py:418
  109.3 3.6 %collective-permute-start.15 = (bf16[2,256,128]{2,1,0:T(8,128)(2,1)}, bf16[2,256,128]{2,1,0:T(8,128)(2,1)S(1)}, u32[]{:S(2)}, u32[]{:S(2)}) collective-permute-start(bf16[2,256,128]{2,1,0:T(8,128)(2,1)} %get-tuple-element.175), channel_id=1, source_target_pairs={{0,1},{1,2},{2,3},{3,4},{4,5},{5,6},{6,7},{7,0},{8,9},{9,10},{10,1... | collective-permute-start | bytes 393224 | tf_op jit(solution)/shard_map/ppermute | solution.py:778
  112.9 11.1 %collective-permute-done.8.refs_2_ = bf16[8,48,256]{2,1,0:T(8,128)(2,1)S(1)} collective-permute-done((bf16[8,48,256]{2,1,0:T(8,128)(2,1)S(1)}, bf16[8,48,256]{2,1,0:T(8,128)(2,1)S(1)}, u32[]{:S(2)}, u32[]{:S(2)}) %collective-permute-start.8) | collective-permute-done | bytes 196640 | tf_op jit(solution)/shard_map/ppermute | solution.py:762
  126.6 5.5 %make_field.3 = (bf16[2,8,192,256]{3,2,1,0:T(8,128)(2,1)}, bf16[8,192,256]{2,1,0:T(8,128)(2,1)}, bf16[2,256,128]{2,1,0:T(8,128)(2,1)}) custom-call(s32[1]{0:T(128)} %bitcast.2.slab, f32[1,2]{1,0:T(1,128)} %weights.3, bf16[2,192,192]{2,1,0:T(8,128)(2,1)} %constant.177.clone.table_y, bf16[512,512]{1,0:T(8,128)(2,1)} %constant.178.clone.table_z, ...), custom_call_target="tpu_custom_call" | custom-call | flops 1409286144 | bytes 3145728 | tf_op jit(solution)/shard_map/make_field/pallas_call | solution.py:418
  138.1 5.1 %go_back.3 = (bf16[8,48,256]{2,1,0:T(8,128)(2,1)}, bf16[8,48,256]{2,1,0:T(8,128)(2,1)}, bf16[8,48,256]{2,1,0:T(8,128)(2,1)}, bf16[8,48,256]{2,1,0:T(8,128)(2,1)}...) custom-call(s32[1]{0:T(128)} %bitcast.2.slab, ...), custom_call_target="tpu_custom_call" | custom-call | flops 1409286144 | bytes 3145728 | tf_op jit(solution)/shard_map/go_back/pallas_call | solution.py:578
  149.5 9.9 %go_back.2 = (bf16[24,32,256]{2,1,0:T(8,128)(2,1)}, bf16[24,32,256]{2,1,0:T(8,128)(2,1)}, bf16[24,32,256]{2,1,0:T(8,128)(2,1)}, bf16[24,32,256]{2,1,0:T(8,128)(2...) custom-call(s32[1]{0:T(128)} %bitcast.2.slab, ...), custom_call_target="tpu_custom_call" | custom-call | flops 2818572288 | bytes 6291456 | tf_op jit(solution)/shard_map/go_back/pallas_call | solution.py:578
  159.4 3.4 %collective-permute-start.25 = (bf16[24,32,256]{2,1,0:T(8,128)(2,1)}, bf16[24,32,256]{2,1,0:T(8,128)(2,1)S(1)}, u32[]{:S(2)}, u32[]{:S(2)}) collective-permute-start(bf16[24,32,256]{2,1,0:T(8,128)(2,1)} %get-tuple-element.202), channel_id=1, source_target_pairs={{0,4},{1,5},{2,6},{3,7},{4,0},{5,1},{6,2},{7,3},{8,12},{9,13},{10,... | collective-permute-start | bytes 1179656 | tf_op jit(solution)/shard_map/ppermute | solution.py:799
  163.5 10.2 %collective-permute-done.19 = bf16[8,48,256]{2,1,0:T(8,128)(2,1)S(1)} collective-permute-done((bf16[8,48,256]{2,1,0:T(8,128)(2,1)}, bf16[8,48,256]{2,1,0:T(8,128)(2,1)S(1)}, u32[]{:S(2)}, u32[]{:S(2)}) %collective-permute-start.19) | collective-permute-done | bytes 196640 | tf_op jit(solution)/shard_map/ppermute | solution.py:799
  173.7 12.1 %collective-permute-start.22 = (bf16[8,48,256]{2,1,0:T(8,128)(2,1)S(1)}, bf16[8,48,256]{2,1,0:T(8,128)(2,1)S(1)}, u32[]{:S(2)}, u32[]{:S(2)}) collective-permute-start(bf16[8,48,256]{2,1,0:T(8,128)(2,1)S(1)} %copy-done.22), channel_id=1, source_target_pairs={{0,6},{1,7},{2,0},{3,1},{4,2},{5,3},{6,4},{7,5},{8,14},{9,15},{10,... | collective-permute-start | bytes 589832 | tf_op jit(solution)/shard_map/ppermute | solution.py:799
  195.1 17.4 %collective-permute-done.22 = bf16[8,48,256]{2,1,0:T(8,128)(2,1)S(1)} collective-permute-done((bf16[8,48,256]{2,1,0:T(8,128)(2,1)S(1)}, bf16[8,48,256]{2,1,0:T(8,128)(2,1)S(1)}, u32[]{:S(2)}, u32[]{:S(2)}) %collective-permute-start.22) | collective-permute-done | bytes 196640 | tf_op jit(solution)/shard_map/ppermute | solution.py:799
  217.2 3.4 %collective-permute-start.30 = (bf16[24,32,256]{2,1,0:T(8,128)(2,1)}, bf16[24,32,256]{2,1,0:T(8,128)(2,1)}, u32[]{:S(2)}, u32[]{:S(2)}) collective-permute-start(bf16[24,32,256]{2,1,0:T(8,128)(2,1)} %get-tuple-element.207), channel_id=1, source_target_pairs={{0,1},{1,2},{2,3},{3,4},{4,5},{5,6},{6,7},{7,0},{8,9},{9,10},{10,1... | collective-permute-start | bytes 1179656 | tf_op jit(solution)/shard_map/ppermute | solution.py:799
  220.7 6.3 %all-reduce.5.cloned.1.call-done = bf16[8,192,256]{2,1,0:T(8,128)(2,1)} async-done(((bf16[8,192,256]{2,1,0:T(8,128)(2,1)}), bf16[8,192,256]{2,1,0:T(8,128)(2,1)}) %all-reduce.5.cloned.1.call-update) | async-done | bytes 786448 | tf_op jit(solution)/shard_map/psum | solution.py:809
  227.0 2.8 %pad_maximum_fusion = bf16[24,192,256]{2,1,0:T(8,128)(2,1)} fusion(bf16[8,192,256]{2,1,0:T(8,128)(2,1)S(1)} %get-tuple-element.222, bf16[8,192,256]{2,1,0:T(8,128)(2,1)} %all-reduce.5.cloned.1.call-done, bf16[8,192,256]{2,1,0:T(8,128)(2,1)S(1)} %get-tuple-element.221), kind=kLoop, calls=%fused_computation | loop fusion | flops 2359296 | bytes 4718592 | tf_op jit(solution)/shard_map/concatenate | solution.py:818
  230.9 11.1 %collective-permute-done.29.refs_5_ = bf16[24,32,256]{2,1,0:T(8,128)(2,1)S(1)} collective-permute-done((bf16[24,32,256]{2,1,0:T(8,128)(2,1)}, bf16[24,32,256]{2,1,0:T(8,128)(2,1)S(1)}, u32[]{:S(2)}, u32[]{:S(2)}) %collective-permute-start.29) | collective-permute-done | bytes 393248 | tf_op jit(solution)/shard_map/ppermute | solution.py:799
  244.5 15.1 %collective-permute-done.31.refs_7_ = bf16[24,32,256]{2,1,0:T(8,128)(2,1)} collective-permute-done((bf16[24,32,256]{2,1,0:T(8,128)(2,1)}, bf16[24,32,256]{2,1,0:T(8,128)(2,1)}, u32[]{:S(2)}, u32[]{:S(2)}) %collective-permute-start.31) | collective-permute-done | bytes 393248 | tf_op jit(solution)/shard_map/ppermute | solution.py:799
  259.6 8.9 %last_x.1 = bf16[2,192,24,256]{3,2,1,0:T(8,128)(2,1)} custom-call(f32[192]{0:T(256)} %constant.183.clone.frequency_x, f32[24,256]{1,0:T(8,128)} %broadcast_add_fusion.frequency_yz, bf16[384,384]{1,0:T(8,128)(2,1)} %dynamic-slice_bitcast_fusion.table, bf16[2,192,24,256]{3,2,1,0:T(8,128)(2,1)} %bitcast.52, bf16[24,32,256]{2,1,0:T(8,128)(2,1)} %get-tuple-element.201.refs_0_, ...), custom_call_target="tpu_custom_call" | custom-call | flops 1811939328 | bytes 14155776 | tf_op jit(solution)/shard_map/last_x/pallas_call | solution.py:636
  (169 shorter events, 56.5 us)
Async XLA Ops:
  7.2 152.2 %all-reduce.3.cloned.1.call-start = ((), (), s32[]{:S(2)}) async-start(), calls=%async_computation | async-start | bytes 3145728 | tf_op jit(solution)/shard_map/psum | solution.py:779
  14.1 27.9 %collective-permute-start.3 = (bf16[24,32,256]{2,1,0:T(8,128)(2,1)}, bf16[24,32,256]{2,1,0:T(8,128)(2,1)S(1)}, u32[]{:S(2)}, u32[]{:S(2)}) collective-permute-start(bf16[24,32,256]{2,1,0:T(8,128)(2,1)} %get-tuple-element.142), channel_id=1, source_target_pairs={{0,4},{1,5},{2,6},{3,7},{4,0},{5,1},{6,2},{7,3},{8,12},{9,13},{10,... | collective-permute-start | bytes 1179656 | tf_op jit(solution)/shard_map/ppermute | solution.py:762
  16.7 34.9 %collective-permute-start.4 = (bf16[24,32,256]{2,1,0:T(8,128)(2,1)}, bf16[24,32,256]{2,1,0:T(8,128)(2,1)S(1)}, u32[]{:S(2)}, u32[]{:S(2)}) collective-permute-start(bf16[24,32,256]{2,1,0:T(8,128)(2,1)} %get-tuple-element.145), channel_id=1, source_target_pairs={{0,5},{1,4},{2,7},{3,6},{4,1},{5,0},{6,3},{7,2},{8,13},{9,12},{10,... | collective-permute-start | bytes 1179656 | tf_op jit(solution)/shard_map/ppermute | solution.py:762
  18.0 45.2 %collective-permute-start.1 = (bf16[24,32,256]{2,1,0:T(8,128)(2,1)}, bf16[24,32,256]{2,1,0:T(8,128)(2,1)S(1)}, u32[]{:S(2)}, u32[]{:S(2)}) collective-permute-start(bf16[24,32,256]{2,1,0:T(8,128)(2,1)} %get-tuple-element.136), channel_id=1, source_target_pairs={{0,2},{1,3},{2,0},{3,1},{4,6},{5,7},{6,4},{7,5},{8,10},{9,11},{10,... | collective-permute-start | bytes 1179656 | tf_op jit(solution)/shard_map/ppermute | solution.py:762
  24.7 39.0 %collective-permute-start.2 = (bf16[24,32,256]{2,1,0:T(8,128)(2,1)}, bf16[24,32,256]{2,1,0:T(8,128)(2,1)S(1)}, u32[]{:S(2)}, u32[]{:S(2)}) collective-permute-start(bf16[24,32,256]{2,1,0:T(8,128)(2,1)} %get-tuple-element.139), channel_id=1, source_target_pairs={{0,3},{1,2},{2,1},{3,0},{4,7},{5,6},{6,5},{7,4},{8,11},{9,10},{10,... | collective-permute-start | bytes 1179656 | tf_op jit(solution)/shard_map/ppermute | solution.py:762
  42.0 34.5 %collective-permute-start.5 = (bf16[24,32,256]{2,1,0:T(8,128)(2,1)}, bf16[24,32,256]{2,1,0:T(8,128)(2,1)S(1)}, u32[]{:S(2)}, u32[]{:S(2)}) collective-permute-start(bf16[24,32,256]{2,1,0:T(8,128)(2,1)} %get-tuple-element.148), channel_id=1, source_target_pairs={{0,6},{1,7},{2,4},{3,5},{4,2},{5,3},{6,0},{7,1},{8,14},{9,15},{10,... | collective-permute-start | bytes 1179656 | tf_op jit(solution)/shard_map/ppermute | solution.py:762
  51.7 33.1 %collective-permute-start.6 = (bf16[24,32,256]{2,1,0:T(8,128)(2,1)}, bf16[24,32,256]{2,1,0:T(8,128)(2,1)S(1)}, u32[]{:S(2)}, u32[]{:S(2)}) collective-permute-start(bf16[24,32,256]{2,1,0:T(8,128)(2,1)} %get-tuple-element.151), channel_id=1, source_target_pairs={{0,7},{1,6},{2,5},{3,4},{4,3},{5,2},{6,1},{7,0},{8,15},{9,14},{10,... | collective-permute-start | bytes 1179656 | tf_op jit(solution)/shard_map/ppermute | solution.py:762
  63.2 36.4 %collective-permute-start.7 = (bf16[8,48,256]{2,1,0:T(8,128)(2,1)}, bf16[8,48,256]{2,1,0:T(8,128)(2,1)S(1)}, u32[]{:S(2)}, u32[]{:S(2)}) collective-permute-start(bf16[8,48,256]{2,1,0:T(8,128)(2,1)} %get-tuple-element.161), channel_id=1, source_target_pairs={{0,1},{1,0},{2,3},{3,2},{4,5},{5,4},{6,7},{7,6},{8,9},{9,8},{10,11... | collective-permute-start | bytes 589832 | tf_op jit(solution)/shard_map/ppermute | solution.py:762
  98.0 128.9 %all-reduce.5.cloned.1.call-start = ((), (), s32[]{:S(2)}) async-start(), calls=%async_computation.1 | async-start | bytes 1572864 | tf_op jit(solution)/shard_map/psum | solution.py:809
  101.6 22.4 %collective-permute-start.8 = (bf16[8,48,256]{2,1,0:T(8,128)(2,1)S(1)}, bf16[8,48,256]{2,1,0:T(8,128)(2,1)S(1)}, u32[]{:S(2)}, u32[]{:S(2)}) collective-permute-start(bf16[8,48,256]{2,1,0:T(8,128)(2,1)S(1)} %copy-done.24), channel_id=1, source_target_pairs={{0,2},{1,3},{2,0},{3,1},{4,6},{5,7},{6,4},{7,5},{8,10},{9,11},{10,... | collective-permute-start | bytes 589832 | tf_op jit(solution)/shard_map/ppermute | solution.py:762
  102.5 21.5 %collective-permute-start.13 = (bf16[8,48,256]{2,1,0:T(8,128)(2,1)S(1)}, bf16[8,48,256]{2,1,0:T(8,128)(2,1)S(1)}, u32[]{:S(2)}, u32[]{:S(2)}) collective-permute-start(bf16[8,48,256]{2,1,0:T(8,128)(2,1)S(1)} %copy-done.23), channel_id=1, source_target_pairs={{0,7},{1,6},{2,5},{3,4},{4,3},{5,2},{6,1},{7,0},{8,15},{9,14},{10,... | collective-permute-start | bytes 589832 | tf_op jit(solution)/shard_map/ppermute | solution.py:762
  105.3 26.8 %collective-permute-start.14 = (bf16[2,256,128]{2,1,0:T(8,128)(2,1)}, bf16[2,256,128]{2,1,0:T(8,128)(2,1)S(1)}, u32[]{:S(2)}, u32[]{:S(2)}) collective-permute-start(bf16[2,256,128]{2,1,0:T(8,128)(2,1)} %get-tuple-element.174), channel_id=1, source_target_pairs={{1,0},{2,1},{3,2},{4,3},{5,4},{6,5},{7,6},{0,7},{9,8},{10,9},{11,1... | collective-permute-start | bytes 393224 | tf_op jit(solution)/shard_map/ppermute | solution.py:777
  109.3 22.9 %collective-permute-start.15 = (bf16[2,256,128]{2,1,0:T(8,128)(2,1)}, bf16[2,256,128]{2,1,0:T(8,128)(2,1)S(1)}, u32[]{:S(2)}, u32[]{:S(2)}) collective-permute-start(bf16[2,256,128]{2,1,0:T(8,128)(2,1)} %get-tuple-element.175), channel_id=1, source_target_pairs={{0,1},{1,2},{2,3},{3,4},{4,5},{5,6},{6,7},{7,0},{8,9},{9,10},{10,1... | collective-permute-start | bytes 393224 | tf_op jit(solution)/shard_map/ppermute | solution.py:778
  143.3 30.4 %collective-permute-start.19 = (bf16[8,48,256]{2,1,0:T(8,128)(2,1)}, bf16[8,48,256]{2,1,0:T(8,128)(2,1)S(1)}, u32[]{:S(2)}, u32[]{:S(2)}) collective-permute-start(bf16[8,48,256]{2,1,0:T(8,128)(2,1)} %get-tuple-element.194), channel_id=1, source_target_pairs={{0,3},{1,4},{2,5},{3,6},{4,7},{5,0},{6,1},{7,2},{8,11},{9,12},{10,... | collective-permute-start | bytes 589832 | tf_op jit(solution)/shard_map/ppermute | solution.py:799
  145.4 40.4 %collective-permute-start.20 = (bf16[8,48,256]{2,1,0:T(8,128)(2,1)}, bf16[8,48,256]{2,1,0:T(8,128)(2,1)S(1)}, u32[]{:S(2)}, u32[]{:S(2)}) collective-permute-start(bf16[8,48,256]{2,1,0:T(8,128)(2,1)} %get-tuple-element.195), channel_id=1, source_target_pairs={{0,5},{1,6},{2,7},{3,0},{4,1},{5,2},{6,3},{7,4},{8,13},{9,14},{10,... | collective-permute-start | bytes 589832 | tf_op jit(solution)/shard_map/ppermute | solution.py:799
  146.3 41.6 %collective-permute-start.21 = (bf16[8,48,256]{2,1,0:T(8,128)(2,1)}, bf16[8,48,256]{2,1,0:T(8,128)(2,1)S(1)}, u32[]{:S(2)}, u32[]{:S(2)}) collective-permute-start(bf16[8,48,256]{2,1,0:T(8,128)(2,1)} %get-tuple-element.196), channel_id=1, source_target_pairs={{0,2},{1,3},{2,4},{3,5},{4,6},{5,7},{6,0},{7,1},{8,10},{9,11},{10,... | collective-permute-start | bytes 589832 | tf_op jit(solution)/shard_map/ppermute | solution.py:799
  159.4 57.8 %collective-permute-start.25 = (bf16[24,32,256]{2,1,0:T(8,128)(2,1)}, bf16[24,32,256]{2,1,0:T(8,128)(2,1)S(1)}, u32[]{:S(2)}, u32[]{:S(2)}) collective-permute-start(bf16[24,32,256]{2,1,0:T(8,128)(2,1)} %get-tuple-element.202), channel_id=1, source_target_pairs={{0,4},{1,5},{2,6},{3,7},{4,0},{5,1},{6,2},{7,3},{8,12},{9,13},{10,... | collective-permute-start | bytes 1179656 | tf_op jit(solution)/shard_map/ppermute | solution.py:799
  162.8 57.8 %collective-permute-start.26 = (bf16[24,32,256]{2,1,0:T(8,128)(2,1)}, bf16[24,32,256]{2,1,0:T(8,128)(2,1)S(1)}, u32[]{:S(2)}, u32[]{:S(2)}) collective-permute-start(bf16[24,32,256]{2,1,0:T(8,128)(2,1)} %get-tuple-element.203), channel_id=1, source_target_pairs={{0,3},{1,4},{2,5},{3,6},{4,7},{5,0},{6,1},{7,2},{8,11},{9,12},{10,... | collective-permute-start | bytes 1179656 | tf_op jit(solution)/shard_map/ppermute | solution.py:799
  173.7 38.8 %collective-permute-start.22 = (bf16[8,48,256]{2,1,0:T(8,128)(2,1)S(1)}, bf16[8,48,256]{2,1,0:T(8,128)(2,1)S(1)}, u32[]{:S(2)}, u32[]{:S(2)}) collective-permute-start(bf16[8,48,256]{2,1,0:T(8,128)(2,1)S(1)} %copy-done.22), channel_id=1, source_target_pairs={{0,6},{1,7},{2,0},{3,1},{4,2},{5,3},{6,4},{7,5},{8,14},{9,15},{10,... | collective-permute-start | bytes 589832 | tf_op jit(solution)/shard_map/ppermute | solution.py:799
  185.8 27.8 %collective-permute-start.23 = (bf16[8,48,256]{2,1,0:T(8,128)(2,1)S(1)}, bf16[8,48,256]{2,1,0:T(8,128)(2,1)S(1)}, u32[]{:S(2)}, u32[]{:S(2)}) collective-permute-start(bf16[8,48,256]{2,1,0:T(8,128)(2,1)S(1)} %copy-done.20), channel_id=1, source_target_pairs={{0,1},{1,2},{2,3},{3,4},{4,5},{5,6},{6,7},{7,0},{8,9},{9,10},{10,1... | collective-permute-start | bytes 589832 | tf_op jit(solution)/shard_map/ppermute | solution.py:799
  187.9 26.5 %collective-permute-start.24 = (bf16[8,48,256]{2,1,0:T(8,128)(2,1)S(1)}, bf16[8,48,256]{2,1,0:T(8,128)(2,1)S(1)}, u32[]{:S(2)}, u32[]{:S(2)}) collective-permute-start(bf16[8,48,256]{2,1,0:T(8,128)(2,1)S(1)} %copy-done.19), channel_id=1, source_target_pairs={{0,7},{1,0},{2,1},{3,2},{4,3},{5,4},{6,5},{7,6},{8,15},{9,8},{10,9... | collective-permute-start | bytes 589832 | tf_op jit(solution)/shard_map/ppermute | solution.py:799
  215.2 26.8 %collective-permute-start.29 = (bf16[24,32,256]{2,1,0:T(8,128)(2,1)}, bf16[24,32,256]{2,1,0:T(8,128)(2,1)S(1)}, u32[]{:S(2)}, u32[]{:S(2)}) collective-permute-start(bf16[24,32,256]{2,1,0:T(8,128)(2,1)} %get-tuple-element.206), channel_id=1, source_target_pairs={{0,6},{1,7},{2,0},{3,1},{4,2},{5,3},{6,4},{7,5},{8,14},{9,15},{10,... | collective-permute-start | bytes 1179656 | tf_op jit(solution)/shard_map/ppermute | solution.py:799
  217.2 27.3 %collective-permute-start.30 = (bf16[24,32,256]{2,1,0:T(8,128)(2,1)}, bf16[24,32,256]{2,1,0:T(8,128)(2,1)}, u32[]{:S(2)}, u32[]{:S(2)}) collective-permute-start(bf16[24,32,256]{2,1,0:T(8,128)(2,1)} %get-tuple-element.207), channel_id=1, source_target_pairs={{0,1},{1,2},{2,3},{3,4},{4,5},{5,6},{6,7},{7,0},{8,9},{9,10},{10,1... | collective-permute-start | bytes 1179656 | tf_op jit(solution)/shard_map/ppermute | solution.py:799
  220.6 39.0 %collective-permute-start.31 = (bf16[24,32,256]{2,1,0:T(8,128)(2,1)}, bf16[24,32,256]{2,1,0:T(8,128)(2,1)}, u32[]{:S(2)}, u32[]{:S(2)}) collective-permute-start(bf16[24,32,256]{2,1,0:T(8,128)(2,1)} %get-tuple-element.208), channel_id=1, source_target_pairs={{0,7},{1,0},{2,1},{3,2},{4,3},{5,4},{6,5},{7,6},{8,15},{9,8},{10,9... | collective-permute-start | bytes 1179656 | tf_op jit(solution)/shard_map/ppermute | solution.py:799
  (45 other events, 863.2 us)
Sparse Core Ops, SparseCore 0:
  98.2 43.7 all-reduce.2
  191.5 35.4 all-reduce.4
where the time goes:
time: 276 us; the launch traced here: 275 us
  waiting for transfers between devices  133 us (48%)
  Pallas kernels  53.8 us (19%)
  starting transfers between devices  53.6 us (19%)
  local copies, waits for them, and re-layouts  16.9 us (6%)
  between operations  14.4 us (5%)
  other arithmetic  3.57 us (1%)
    ppermute x14, waiting for transfers between devices, send(): return lax.ppermute(block, 'fft', [(j, j ^ k) for j in range(pieces)])  69.1 us
    ppermute x14, waiting for transfers between devices, permute_all(): received.append(lax.ppermute(block, 'fft', pairs))  57.7 us
    ppermute x14, starting transfers between devices, permute_all(): received.append(lax.ppermute(block, 'fft', pairs))  29.6 us
    ppermute x14, starting transfers between devices, send(): return lax.ppermute(block, 'fft', [(j, j ^ k) for j in range(pieces)])  15.8 us
    pallas_call x2, Pallas kernels, make_field(): pl.pallas_call(functools.partial(field_kernel, pieces=pieces, count=len(b...  15.6 us
    pallas_call x2, Pallas kernels, go_back(): pl.pallas_call(functools.partial(back_kernel, pieces=pieces, natural=natu...  14.9 us
    pallas_call x2, Pallas kernels, first_x(): pl.pallas_call(functools.partial(first_x_kernel, pieces=pieces, natural=n...  12 us
    pallas_call x1, Pallas kernels, last_x(): pl.pallas_call(last_x_kernel, grid=(2,), in_specs=[SMEM_SPEC, pl.BlockSpe...  8.92 us
  transfers between devices with their start and end apart: 34, of which 16 were waited for; matrix products, arithmetic and copies ran while one was open for 7% of the time, Pallas kernels for 14%

commit v1 on v0

--- a/solution.py
+++ b/solution.py
@@ -718,7 +718,7 @@
     section_outer, table_x_inner, sphere_blocks = lax.optimization_barrier(
         (section_outer, table_x_inner, sphere_blocks)
     )
-    section_inner = first_x(where, table_x_inner, coeffs, len(inner), pieces, True)
+    section_inner = first_x(where, table_x_inner, coeffs, len(inner), pieces, False)
 
     entries = atom_dev * blocks
 
@@ -778,8 +778,8 @@
     from_previous = lax.ppermute(to_following, "fft", up)
     density_outer = lax.psum(density_outer, "band")
     wave_inner, density_inner, rows_inner = make_field(
-        where, occupation, received_inner, table_y_inner, table_z, rows_codes[1],
-        sides_inner, len(inner), pieces, True,
+        where, occupation, received_inner, table_y_outer, table_z, rows_codes[1],
+        sides_inner, len(inner), pieces, False,
     )
     projected, spread = make_nonlocal(
         coupled, projectors, [rows_outer, rows_inner, from_following, from_previous]
@@ -789,8 +789,8 @@
     edge_steps = EDGE // PLANES
     inner_steps = len(inner) // PLANES
     back_inner = go_back(
-        where, wave_inner, potential, table_back_z, table_back_y_inner, lane_codes[1],
-        sides_inner, [spread], lambda i: i + edge_steps, pieces, True,
+        where, wave_inner, potential, table_back_z, table_back_y_outer, lane_codes[1],
+        sides_inner, [spread], lambda i: i + edge_steps, pieces, False,
     )
     def permute_all(values):
         received = [values[0]]
@@ -809,12 +809,6 @@
     density_inner = lax.psum(density_inner, "band")
     back_outer, density_outer = lax.optimization_barrier((back_outer, density_outer))
     back_outer = permute_all(back_outer)
-    back_inner = [
-        b.reshape(len(inner), 2, 2, columns // 2, size_z)
-        .transpose(3, 1, 2, 0, 4)
-        .reshape(columns, -1, size_z)
-        for b in back_inner
-    ]
     density = jnp.concatenate([density_outer[:EDGE], density_inner, density_outer[EDGE:]], axis=0)
 
     index_x = np.arange(size_x)

time: 276 us -> 272 us (0.986)
  local copies, waits for them, and re-layouts: 16.9 us -> 12.3 us
    transpose x8 -> x0, local copies, waits for them, and re-layouts: 5.62 us -> none  [per_device_chunked(): back_inner = [b.reshape(len(inner), 2, 2, columns // 2, size_z).transpose...]
    ppermute x14, waiting for transfers between devices: 57.7 us -> 63.1 us  [permute_all(): received.append(lax.ppermute(block, 'fft', pairs))]
    psum x1, waiting for transfers between devices: 6.26 us -> 0.98 us  [per_device_chunked(): density_inner = lax.psum(density_inner, 'band')]
  transfers between devices with their start and end apart: 34 -> 34, of which waited for: 16 -> 16; matrix products, arithmetic and copies ran while one was open for 7% -> 5% of each run, Pallas kernels for 14% -> 14%
where the time goes in v1:
time: 272 us; the launch traced here: 271 us
  waiting for transfers between devices  134 us (49%)
  Pallas kernels  54.1 us (20%)
  starting transfers between devices  53.6 us (20%)
  between operations  14.4 us (5%)
  local copies, waits for them, and re-layouts  12.3 us (5%)
  other arithmetic  3.58 us (1%)
    ppermute x14, waiting for transfers between devices, send(): return lax.ppermute(block, 'fft', [(j, j ^ k) for j in range(pieces)])  69.4 us
    ppermute x14, waiting for transfers between devices, permute_all(): received.append(lax.ppermute(block, 'fft', pairs))  63.1 us
    ppermute x14, starting transfers between devices, permute_all(): received.append(lax.ppermute(block, 'fft', pairs))  29.6 us
    ppermute x14, starting transfers between devices, send(): return lax.ppermute(block, 'fft', [(j, j ^ k) for j in range(pieces)])  15.9 us
    pallas_call x2, Pallas kernels, make_field(): pl.pallas_call(functools.partial(field_kernel, pieces=pieces, count=len(b...  15.8 us
    pallas_call x2, Pallas kernels, go_back(): pl.pallas_call(functools.partial(back_kernel, pieces=pieces, natural=natu...  15.4 us
    pallas_call x2, Pallas kernels, first_x(): pl.pallas_call(functools.partial(first_x_kernel, pieces=pieces, natural=n...  11.6 us
    pallas_call x1, Pallas kernels, last_x(): pl.pallas_call(last_x_kernel, grid=(2,), in_specs=[SMEM_SPEC, pl.BlockSpe...  8.93 us
  transfers between devices with their start and end apart: 34, of which 16 were waited for; matrix products, arithmetic and copies ran while one was open for 5% of the time, Pallas kernels for 14%

profile of v1, /device:TPU:10, one launch (start us, length us, event | category | flops | bytes accessed | tf_op | source)
XLA Modules:
  0.0 271.5 jit_solution(9947533360354697918)
XLA Ops:
  7.2 6.3 %first_x.2 = (bf16[24,32,256]{2,1,0:T(8,128)(2,1)}, bf16[24,32,256]{2,1,0:T(8,128)(2,1)}, bf16[24,32,256]{2,1,0:T(8,128)(2,1)}, bf16[24,32,256]{2,1,0:T(8,128)(2...) custom-call(s32[1]{0:T(128)} %bitcast.2.slab, ...), custom_call_target="tpu_custom_call" | custom-call | flops 1207959552 | bytes 9437184 | tf_op jit(solution)/shard_map/first_x/pallas_call | solution.py:274
  18.6 6.1 %collective-permute-done.refs_1_ = bf16[24,32,256]{2,1,0:T(8,128)(2,1)S(1)} collective-permute-done((bf16[24,32,256]{2,1,0:T(8,128)(2,1)}, bf16[24,32,256]{2,1,0:T(8,128)(2,1)S(1)}, u32[]{:S(2)}, u32[]{:S(2)}) %collective-permute-start) | collective-permute-done | bytes 393248 | tf_op jit(solution)/shard_map/ppermute | solution.py:762
  24.8 17.2 %collective-permute-done.3.refs_4_ = bf16[24,32,256]{2,1,0:T(8,128)(2,1)S(1)} collective-permute-done((bf16[24,32,256]{2,1,0:T(8,128)(2,1)}, bf16[24,32,256]{2,1,0:T(8,128)(2,1)S(1)}, u32[]{:S(2)}, u32[]{:S(2)}) %collective-permute-start.3) | collective-permute-done | bytes 393248 | tf_op jit(solution)/shard_map/ppermute | solution.py:762
  42.4 9.2 %collective-permute-done.4.refs_5_ = bf16[24,32,256]{2,1,0:T(8,128)(2,1)S(1)} collective-permute-done((bf16[24,32,256]{2,1,0:T(8,128)(2,1)}, bf16[24,32,256]{2,1,0:T(8,128)(2,1)S(1)}, u32[]{:S(2)}, u32[]{:S(2)}) %collective-permute-start.4) | collective-permute-done | bytes 393248 | tf_op jit(solution)/shard_map/ppermute | solution.py:762
  54.9 5.3 %first_x.3 = (bf16[24,16,256]{2,1,0:T(8,128)(2,1)}, bf16[24,16,256]{2,1,0:T(8,128)(2,1)}, bf16[24,16,256]{2,1,0:T(8,128)(2,1)}, bf16[24,16,256]{2,1,0:T(8,128)(2...) custom-call(s32[1]{0:T(128)} %bitcast.2.slab, ...), custom_call_target="tpu_custom_call" | custom-call | flops 603979776 | bytes 9437184 | tf_op jit(solution)/shard_map/first_x/pallas_call | solution.py:274
  63.3 13.1 %collective-permute-done.5.refs_6_ = bf16[24,32,256]{2,1,0:T(8,128)(2,1)S(1)} collective-permute-done((bf16[24,32,256]{2,1,0:T(8,128)(2,1)}, bf16[24,32,256]{2,1,0:T(8,128)(2,1)S(1)}, u32[]{:S(2)}, u32[]{:S(2)}) %collective-permute-start.5) | collective-permute-done | bytes 393248 | tf_op jit(solution)/shard_map/ppermute | solution.py:762
  76.5 8.3 %collective-permute-done.6.refs_7_ = bf16[24,32,256]{2,1,0:T(8,128)(2,1)S(1)} collective-permute-done((bf16[24,32,256]{2,1,0:T(8,128)(2,1)}, bf16[24,32,256]{2,1,0:T(8,128)(2,1)S(1)}, u32[]{:S(2)}, u32[]{:S(2)}) %collective-permute-start.6) | collective-permute-done | bytes 393248 | tf_op jit(solution)/shard_map/ppermute | solution.py:762
  84.7 3.1 %collective-permute-start.10 = (bf16[24,16,256]{2,1,0:T(8,128)(2,1)}, bf16[24,16,256]{2,1,0:T(8,128)(2,1)S(1)}, u32[]{:S(2)}, u32[]{:S(2)}) collective-permute-start(bf16[24,16,256]{2,1,0:T(8,128)(2,1)} %get-tuple-element.166), channel_id=1, source_target_pairs={{0,4},{1,5},{2,6},{3,7},{4,0},{5,1},{6,2},{7,3},{8,12},{9,13},{10,... | collective-permute-start | bytes 589832 | tf_op jit(solution)/shard_map/ppermute | solution.py:762
  87.9 10.1 %make_field.2 = (bf16[2,16,192,256]{3,2,1,0:T(8,128)(2,1)}, bf16[16,192,256]{2,1,0:T(8,128)(2,1)}, bf16[2,256,128]{2,1,0:T(8,128)(2,1)}, bf16[2,256,128]{2,1,0:T(8,128)(2,1)}, bf16[2,256,128]{2,1,0:T(8,128)(2,1)}) custom-call(s32[1]{0:T(128)} %bitcast.2.slab, f32[1,2]{1,0:T(1,128)} %weights.3, bf16[2,192,192]{2,1,0:T(8,128)(2,1)} %constant.172.clone.table_y, ...), custom_call_target="tpu_custom_call" | custom-call | flops 2818572288 | bytes 6291456 | tf_op jit(solution)/shard_map/make_field/pallas_call | solution.py:418
  109.3 3.6 %collective-permute-start.15 = (bf16[2,256,128]{2,1,0:T(8,128)(2,1)}, bf16[2,256,128]{2,1,0:T(8,128)(2,1)S(1)}, u32[]{:S(2)}, u32[]{:S(2)}) collective-permute-start(bf16[2,256,128]{2,1,0:T(8,128)(2,1)} %get-tuple-element.175), channel_id=1, source_target_pairs={{0,1},{1,2},{2,3},{3,4},{4,5},{5,6},{6,7},{7,0},{8,9},{9,10},{10,1... | collective-permute-start | bytes 393224 | tf_op jit(solution)/shard_map/ppermute | solution.py:778
  112.9 11.0 %collective-permute-done.8.refs_2_ = bf16[24,16,256]{2,1,0:T(8,128)(2,1)S(1)} collective-permute-done((bf16[24,16,256]{2,1,0:T(8,128)(2,1)S(1)}, bf16[24,16,256]{2,1,0:T(8,128)(2,1)S(1)}, u32[]{:S(2)}, u32[]{:S(2)}) %collective-permute-start.8) | collective-permute-done | bytes 196640 | tf_op jit(solution)/shard_map/ppermute | solution.py:762
  126.6 5.7 %make_field.3 = (bf16[2,8,192,256]{3,2,1,0:T(8,128)(2,1)}, bf16[8,192,256]{2,1,0:T(8,128)(2,1)}, bf16[2,256,128]{2,1,0:T(8,128)(2,1)}) custom-call(s32[1]{0:T(128)} %bitcast.2.slab, f32[1,2]{1,0:T(1,128)} %weights.3, bf16[2,192,192]{2,1,0:T(8,128)(2,1)} %constant.172.clone.table_y, bf16[512,512]{1,0:T(8,128)(2,1)} %constant.173.clone.table_z, ...), custom_call_target="tpu_custom_call" | custom-call | flops 1409286144 | bytes 3145728 | tf_op jit(solution)/shard_map/make_field/pallas_call | solution.py:418
  138.3 5.5 %go_back.3 = (bf16[24,16,256]{2,1,0:T(8,128)(2,1)}, bf16[24,16,256]{2,1,0:T(8,128)(2,1)}, bf16[24,16,256]{2,1,0:T(8,128)(2,1)}, bf16[24,16,256]{2,1,0:T(8,128)(2...) custom-call(s32[1]{0:T(128)} %bitcast.2.slab, ...), custom_call_target="tpu_custom_call" | custom-call | flops 1409286144 | bytes 3145728 | tf_op jit(solution)/shard_map/go_back/pallas_call | solution.py:578
  150.2 9.8 %go_back.2 = (bf16[24,32,256]{2,1,0:T(8,128)(2,1)}, bf16[24,32,256]{2,1,0:T(8,128)(2,1)}, bf16[24,32,256]{2,1,0:T(8,128)(2,1)}, bf16[24,32,256]{2,1,0:T(8,128)(2...) custom-call(s32[1]{0:T(128)} %bitcast.2.slab, ...), custom_call_target="tpu_custom_call" | custom-call | flops 2818572288 | bytes 6291456 | tf_op jit(solution)/shard_map/go_back/pallas_call | solution.py:578
  160.0 3.3 %collective-permute-start.25 = (bf16[24,32,256]{2,1,0:T(8,128)(2,1)}, bf16[24,32,256]{2,1,0:T(8,128)(2,1)S(1)}, u32[]{:S(2)}, u32[]{:S(2)}) collective-permute-start(bf16[24,32,256]{2,1,0:T(8,128)(2,1)} %get-tuple-element.202), channel_id=1, source_target_pairs={{0,4},{1,5},{2,6},{3,7},{4,0},{5,1},{6,2},{7,3},{8,12},{9,13},{10,... | collective-permute-start | bytes 1179656 | tf_op jit(solution)/shard_map/ppermute | solution.py:799
  164.2 10.0 %collective-permute-done.19.refs_10_ = bf16[24,16,256]{2,1,0:T(8,128)(2,1)S(1)} collective-permute-done((bf16[24,16,256]{2,1,0:T(8,128)(2,1)}, bf16[24,16,256]{2,1,0:T(8,128)(2,1)S(1)}, u32[]{:S(2)}, u32[]{:S(2)}) %collective-permute-start.19) | collective-permute-done | bytes 196640 | tf_op jit(solution)/shard_map/ppermute | solution.py:799
  174.1 12.3 %collective-permute-start.22 = (bf16[24,16,256]{2,1,0:T(8,128)(2,1)S(1)}, bf16[24,16,256]{2,1,0:T(8,128)(2,1)S(1)}, u32[]{:S(2)}, u32[]{:S(2)}) collective-permute-start(bf16[24,16,256]{2,1,0:T(8,128)(2,1)S(1)} %copy-done.31), channel_id=1, source_target_pairs={{0,6},{1,7},{2,0},{3,1},{4,2},{5,3},{6,4},{7,5},{8,14},{9,15},{10,... | collective-permute-start | bytes 589832 | tf_op jit(solution)/shard_map/ppermute | solution.py:799
  191.1 21.2 %collective-permute-done.22.refs_13_ = bf16[24,16,256]{2,1,0:T(8,128)(2,1)S(1)} collective-permute-done((bf16[24,16,256]{2,1,0:T(8,128)(2,1)S(1)}, bf16[24,16,256]{2,1,0:T(8,128)(2,1)S(1)}, u32[]{:S(2)}, u32[]{:S(2)}) %collective-permute-start.22) | collective-permute-done | bytes 196640 | tf_op jit(solution)/shard_map/ppermute | solution.py:799
  212.4 6.0 %collective-permute-done.23.refs_14_ = bf16[24,16,256]{2,1,0:T(8,128)(2,1)S(1)} collective-permute-done((bf16[24,16,256]{2,1,0:T(8,128)(2,1)S(1)}, bf16[24,16,256]{2,1,0:T(8,128)(2,1)S(1)}, u32[]{:S(2)}, u32[]{:S(2)}) %collective-permute-start.23) | collective-permute-done | bytes 196640 | tf_op jit(solution)/shard_map/ppermute | solution.py:799
  220.4 3.9 %collective-permute-start.30 = (bf16[24,32,256]{2,1,0:T(8,128)(2,1)}, bf16[24,32,256]{2,1,0:T(8,128)(2,1)}, u32[]{:S(2)}, u32[]{:S(2)}) collective-permute-start(bf16[24,32,256]{2,1,0:T(8,128)(2,1)} %get-tuple-element.207), channel_id=1, source_target_pairs={{0,1},{1,2},{2,3},{3,4},{4,5},{5,6},{6,7},{7,0},{8,9},{9,10},{10,1... | collective-permute-start | bytes 1179656 | tf_op jit(solution)/shard_map/ppermute | solution.py:799
  232.2 4.0 %collective-permute-done.28.refs_4_ = bf16[24,32,256]{2,1,0:T(8,128)(2,1)S(1)} collective-permute-done((bf16[24,32,256]{2,1,0:T(8,128)(2,1)}, bf16[24,32,256]{2,1,0:T(8,128)(2,1)S(1)}, u32[]{:S(2)}, u32[]{:S(2)}) %collective-permute-start.28) | collective-permute-done | bytes 393248 | tf_op jit(solution)/shard_map/ppermute | solution.py:799
  236.2 10.5 %collective-permute-done.29.refs_5_ = bf16[24,32,256]{2,1,0:T(8,128)(2,1)S(1)} collective-permute-done((bf16[24,32,256]{2,1,0:T(8,128)(2,1)}, bf16[24,32,256]{2,1,0:T(8,128)(2,1)S(1)}, u32[]{:S(2)}, u32[]{:S(2)}) %collective-permute-start.29) | collective-permute-done | bytes 393248 | tf_op jit(solution)/shard_map/ppermute | solution.py:799
  246.7 9.0 %collective-permute-done.31.refs_7_ = bf16[24,32,256]{2,1,0:T(8,128)(2,1)} collective-permute-done((bf16[24,32,256]{2,1,0:T(8,128)(2,1)}, bf16[24,32,256]{2,1,0:T(8,128)(2,1)}, u32[]{:S(2)}, u32[]{:S(2)}) %collective-permute-start.31) | collective-permute-done | bytes 393248 | tf_op jit(solution)/shard_map/ppermute | solution.py:799
  255.7 8.9 %last_x.1 = bf16[2,192,24,256]{3,2,1,0:T(8,128)(2,1)} custom-call(f32[192]{0:T(256)} %constant.177.clone.frequency_x, f32[24,256]{1,0:T(8,128)} %broadcast_add_fusion.frequency_yz, bf16[384,384]{1,0:T(8,128)(2,1)} %dynamic-slice_bitcast_fusion.table, bf16[2,192,24,256]{3,2,1,0:T(8,128)(2,1)} %bitcast.20, bf16[24,32,256]{2,1,0:T(8,128)(2,1)} %get-tuple-element.201.refs_0_, ...), custom_call_target="tpu_custom_call" | custom-call | flops 1811939328 | bytes 14155776 | tf_op jit(solution)/shard_map/last_x/pallas_call | solution.py:636
  (163 shorter events, 53.5 us)
Async XLA Ops:
  7.2 152.9 %all-reduce.3.cloned.1.call-start = ((), (), s32[]{:S(2)}) async-start(), calls=%async_computation | async-start | bytes 3145728 | tf_op jit(solution)/shard_map/psum | solution.py:779
  14.1 27.9 %collective-permute-start.3 = (bf16[24,32,256]{2,1,0:T(8,128)(2,1)}, bf16[24,32,256]{2,1,0:T(8,128)(2,1)S(1)}, u32[]{:S(2)}, u32[]{:S(2)}) collective-permute-start(bf16[24,32,256]{2,1,0:T(8,128)(2,1)} %get-tuple-element.142), channel_id=1, source_target_pairs={{0,4},{1,5},{2,6},{3,7},{4,0},{5,1},{6,2},{7,3},{8,12},{9,13},{10,... | collective-permute-start | bytes 1179656 | tf_op jit(solution)/shard_map/ppermute | solution.py:762
  16.7 34.9 %collective-permute-start.4 = (bf16[24,32,256]{2,1,0:T(8,128)(2,1)}, bf16[24,32,256]{2,1,0:T(8,128)(2,1)S(1)}, u32[]{:S(2)}, u32[]{:S(2)}) collective-permute-start(bf16[24,32,256]{2,1,0:T(8,128)(2,1)} %get-tuple-element.145), channel_id=1, source_target_pairs={{0,5},{1,4},{2,7},{3,6},{4,1},{5,0},{6,3},{7,2},{8,13},{9,12},{10,... | collective-permute-start | bytes 1179656 | tf_op jit(solution)/shard_map/ppermute | solution.py:762
  18.0 44.9 %collective-permute-start.1 = (bf16[24,32,256]{2,1,0:T(8,128)(2,1)}, bf16[24,32,256]{2,1,0:T(8,128)(2,1)S(1)}, u32[]{:S(2)}, u32[]{:S(2)}) collective-permute-start(bf16[24,32,256]{2,1,0:T(8,128)(2,1)} %get-tuple-element.136), channel_id=1, source_target_pairs={{0,2},{1,3},{2,0},{3,1},{4,6},{5,7},{6,4},{7,5},{8,10},{9,11},{10,... | collective-permute-start | bytes 1179656 | tf_op jit(solution)/shard_map/ppermute | solution.py:762
  24.6 38.7 %collective-permute-start.2 = (bf16[24,32,256]{2,1,0:T(8,128)(2,1)}, bf16[24,32,256]{2,1,0:T(8,128)(2,1)S(1)}, u32[]{:S(2)}, u32[]{:S(2)}) collective-permute-start(bf16[24,32,256]{2,1,0:T(8,128)(2,1)} %get-tuple-element.139), channel_id=1, source_target_pairs={{0,3},{1,2},{2,1},{3,0},{4,7},{5,6},{6,5},{7,4},{8,11},{9,10},{10,... | collective-permute-start | bytes 1179656 | tf_op jit(solution)/shard_map/ppermute | solution.py:762
  42.0 34.5 %collective-permute-start.5 = (bf16[24,32,256]{2,1,0:T(8,128)(2,1)}, bf16[24,32,256]{2,1,0:T(8,128)(2,1)S(1)}, u32[]{:S(2)}, u32[]{:S(2)}) collective-permute-start(bf16[24,32,256]{2,1,0:T(8,128)(2,1)} %get-tuple-element.148), channel_id=1, source_target_pairs={{0,6},{1,7},{2,4},{3,5},{4,2},{5,3},{6,0},{7,1},{8,14},{9,15},{10,... | collective-permute-start | bytes 1179656 | tf_op jit(solution)/shard_map/ppermute | solution.py:762
  51.6 33.1 %collective-permute-start.6 = (bf16[24,32,256]{2,1,0:T(8,128)(2,1)}, bf16[24,32,256]{2,1,0:T(8,128)(2,1)S(1)}, u32[]{:S(2)}, u32[]{:S(2)}) collective-permute-start(bf16[24,32,256]{2,1,0:T(8,128)(2,1)} %get-tuple-element.151), channel_id=1, source_target_pairs={{0,7},{1,6},{2,5},{3,4},{4,3},{5,2},{6,1},{7,0},{8,15},{9,14},{10,... | collective-permute-start | bytes 1179656 | tf_op jit(solution)/shard_map/ppermute | solution.py:762
  62.9 36.8 %collective-permute-start.7 = (bf16[24,16,256]{2,1,0:T(8,128)(2,1)}, bf16[24,16,256]{2,1,0:T(8,128)(2,1)S(1)}, u32[]{:S(2)}, u32[]{:S(2)}) collective-permute-start(bf16[24,16,256]{2,1,0:T(8,128)(2,1)} %get-tuple-element.161), channel_id=1, source_target_pairs={{0,1},{1,0},{2,3},{3,2},{4,5},{5,4},{6,7},{7,6},{8,9},{9,8},{10,11... | collective-permute-start | bytes 589832 | tf_op jit(solution)/shard_map/ppermute | solution.py:762
  98.0 128.9 %all-reduce.5.cloned.1.call-start = ((), (), s32[]{:S(2)}) async-start(), calls=%async_computation.1 | async-start | bytes 1572864 | tf_op jit(solution)/shard_map/psum | solution.py:809
  101.6 22.4 %collective-permute-start.8 = (bf16[24,16,256]{2,1,0:T(8,128)(2,1)S(1)}, bf16[24,16,256]{2,1,0:T(8,128)(2,1)S(1)}, u32[]{:S(2)}, u32[]{:S(2)}) collective-permute-start(bf16[24,16,256]{2,1,0:T(8,128)(2,1)S(1)} %copy-done.26), channel_id=1, source_target_pairs={{0,2},{1,3},{2,0},{3,1},{4,6},{5,7},{6,4},{7,5},{8,10},{9,11},{10,... | collective-permute-start | bytes 589832 | tf_op jit(solution)/shard_map/ppermute | solution.py:762
  102.5 21.5 %collective-permute-start.13 = (bf16[24,16,256]{2,1,0:T(8,128)(2,1)S(1)}, bf16[24,16,256]{2,1,0:T(8,128)(2,1)S(1)}, u32[]{:S(2)}, u32[]{:S(2)}) collective-permute-start(bf16[24,16,256]{2,1,0:T(8,128)(2,1)S(1)} %copy-done.25), channel_id=1, source_target_pairs={{0,7},{1,6},{2,5},{3,4},{4,3},{5,2},{6,1},{7,0},{8,15},{9,14},{10,... | collective-permute-start | bytes 589832 | tf_op jit(solution)/shard_map/ppermute | solution.py:762
  105.3 27.1 %collective-permute-start.14 = (bf16[2,256,128]{2,1,0:T(8,128)(2,1)}, bf16[2,256,128]{2,1,0:T(8,128)(2,1)S(1)}, u32[]{:S(2)}, u32[]{:S(2)}) collective-permute-start(bf16[2,256,128]{2,1,0:T(8,128)(2,1)} %get-tuple-element.174), channel_id=1, source_target_pairs={{1,0},{2,1},{3,2},{4,3},{5,4},{6,5},{7,6},{0,7},{9,8},{10,9},{11,1... | collective-permute-start | bytes 393224 | tf_op jit(solution)/shard_map/ppermute | solution.py:777
  109.3 23.1 %collective-permute-start.15 = (bf16[2,256,128]{2,1,0:T(8,128)(2,1)}, bf16[2,256,128]{2,1,0:T(8,128)(2,1)S(1)}, u32[]{:S(2)}, u32[]{:S(2)}) collective-permute-start(bf16[2,256,128]{2,1,0:T(8,128)(2,1)} %get-tuple-element.175), channel_id=1, source_target_pairs={{0,1},{1,2},{2,3},{3,4},{4,5},{5,6},{6,7},{7,0},{8,9},{9,10},{10,1... | collective-permute-start | bytes 393224 | tf_op jit(solution)/shard_map/ppermute | solution.py:778
  143.9 30.3 %collective-permute-start.19 = (bf16[24,16,256]{2,1,0:T(8,128)(2,1)}, bf16[24,16,256]{2,1,0:T(8,128)(2,1)S(1)}, u32[]{:S(2)}, u32[]{:S(2)}) collective-permute-start(bf16[24,16,256]{2,1,0:T(8,128)(2,1)} %get-tuple-element.194), channel_id=1, source_target_pairs={{0,3},{1,4},{2,5},{3,6},{4,7},{5,0},{6,1},{7,2},{8,11},{9,12},{10,... | collective-permute-start | bytes 589832 | tf_op jit(solution)/shard_map/ppermute | solution.py:799
  146.1 40.4 %collective-permute-start.20 = (bf16[24,16,256]{2,1,0:T(8,128)(2,1)}, bf16[24,16,256]{2,1,0:T(8,128)(2,1)S(1)}, u32[]{:S(2)}, u32[]{:S(2)}) collective-permute-start(bf16[24,16,256]{2,1,0:T(8,128)(2,1)} %get-tuple-element.195), channel_id=1, source_target_pairs={{0,5},{1,6},{2,7},{3,0},{4,1},{5,2},{6,3},{7,4},{8,13},{9,14},{10,... | collective-permute-start | bytes 589832 | tf_op jit(solution)/shard_map/ppermute | solution.py:799
  146.8 41.7 %collective-permute-start.21 = (bf16[24,16,256]{2,1,0:T(8,128)(2,1)}, bf16[24,16,256]{2,1,0:T(8,128)(2,1)S(1)}, u32[]{:S(2)}, u32[]{:S(2)}) collective-permute-start(bf16[24,16,256]{2,1,0:T(8,128)(2,1)} %get-tuple-element.196), channel_id=1, source_target_pairs={{0,2},{1,3},{2,4},{3,5},{4,6},{5,7},{6,0},{7,1},{8,10},{9,11},{10,... | collective-permute-start | bytes 589832 | tf_op jit(solution)/shard_map/ppermute | solution.py:799
  160.0 60.4 %collective-permute-start.25 = (bf16[24,32,256]{2,1,0:T(8,128)(2,1)}, bf16[24,32,256]{2,1,0:T(8,128)(2,1)S(1)}, u32[]{:S(2)}, u32[]{:S(2)}) collective-permute-start(bf16[24,32,256]{2,1,0:T(8,128)(2,1)} %get-tuple-element.202), channel_id=1, source_target_pairs={{0,4},{1,5},{2,6},{3,7},{4,0},{5,1},{6,2},{7,3},{8,12},{9,13},{10,... | collective-permute-start | bytes 1179656 | tf_op jit(solution)/shard_map/ppermute | solution.py:799
  163.4 60.9 %collective-permute-start.26 = (bf16[24,32,256]{2,1,0:T(8,128)(2,1)}, bf16[24,32,256]{2,1,0:T(8,128)(2,1)S(1)}, u32[]{:S(2)}, u32[]{:S(2)}) collective-permute-start(bf16[24,32,256]{2,1,0:T(8,128)(2,1)} %get-tuple-element.203), channel_id=1, source_target_pairs={{0,3},{1,4},{2,5},{3,6},{4,7},{5,0},{6,1},{7,2},{8,11},{9,12},{10,... | collective-permute-start | bytes 1179656 | tf_op jit(solution)/shard_map/ppermute | solution.py:799
  174.1 38.3 %collective-permute-start.22 = (bf16[24,16,256]{2,1,0:T(8,128)(2,1)S(1)}, bf16[24,16,256]{2,1,0:T(8,128)(2,1)S(1)}, u32[]{:S(2)}, u32[]{:S(2)}) collective-permute-start(bf16[24,16,256]{2,1,0:T(8,128)(2,1)S(1)} %copy-done.31), channel_id=1, source_target_pairs={{0,6},{1,7},{2,0},{3,1},{4,2},{5,3},{6,4},{7,5},{8,14},{9,15},{10,... | collective-permute-start | bytes 589832 | tf_op jit(solution)/shard_map/ppermute | solution.py:799
  186.5 31.9 %collective-permute-start.23 = (bf16[24,16,256]{2,1,0:T(8,128)(2,1)S(1)}, bf16[24,16,256]{2,1,0:T(8,128)(2,1)S(1)}, u32[]{:S(2)}, u32[]{:S(2)}) collective-permute-start(bf16[24,16,256]{2,1,0:T(8,128)(2,1)S(1)} %copy-done.30), channel_id=1, source_target_pairs={{0,1},{1,2},{2,3},{3,4},{4,5},{5,6},{6,7},{7,0},{8,9},{9,10},{10,1... | collective-permute-start | bytes 589832 | tf_op jit(solution)/shard_map/ppermute | solution.py:799
  188.5 29.8 %collective-permute-start.24 = (bf16[24,16,256]{2,1,0:T(8,128)(2,1)S(1)}, bf16[24,16,256]{2,1,0:T(8,128)(2,1)S(1)}, u32[]{:S(2)}, u32[]{:S(2)}) collective-permute-start(bf16[24,16,256]{2,1,0:T(8,128)(2,1)S(1)} %copy-done.27), channel_id=1, source_target_pairs={{0,7},{1,0},{2,1},{3,2},{4,3},{5,4},{6,5},{7,6},{8,15},{9,8},{10,9... | collective-permute-start | bytes 589832 | tf_op jit(solution)/shard_map/ppermute | solution.py:799
  218.4 28.3 %collective-permute-start.29 = (bf16[24,32,256]{2,1,0:T(8,128)(2,1)}, bf16[24,32,256]{2,1,0:T(8,128)(2,1)S(1)}, u32[]{:S(2)}, u32[]{:S(2)}) collective-permute-start(bf16[24,32,256]{2,1,0:T(8,128)(2,1)} %get-tuple-element.206), channel_id=1, source_target_pairs={{0,6},{1,7},{2,0},{3,1},{4,2},{5,3},{6,4},{7,5},{8,14},{9,15},{10,... | collective-permute-start | bytes 1179656 | tf_op jit(solution)/shard_map/ppermute | solution.py:799
  220.4 26.3 %collective-permute-start.30 = (bf16[24,32,256]{2,1,0:T(8,128)(2,1)}, bf16[24,32,256]{2,1,0:T(8,128)(2,1)}, u32[]{:S(2)}, u32[]{:S(2)}) collective-permute-start(bf16[24,32,256]{2,1,0:T(8,128)(2,1)} %get-tuple-element.207), channel_id=1, source_target_pairs={{0,1},{1,2},{2,3},{3,4},{4,5},{5,6},{6,7},{7,0},{8,9},{9,10},{10,1... | collective-permute-start | bytes 1179656 | tf_op jit(solution)/shard_map/ppermute | solution.py:799
  224.3 31.3 %collective-permute-start.31 = (bf16[24,32,256]{2,1,0:T(8,128)(2,1)}, bf16[24,32,256]{2,1,0:T(8,128)(2,1)}, u32[]{:S(2)}, u32[]{:S(2)}) collective-permute-start(bf16[24,32,256]{2,1,0:T(8,128)(2,1)} %get-tuple-element.208), channel_id=1, source_target_pairs={{0,7},{1,0},{2,1},{3,2},{4,3},{5,4},{6,5},{7,6},{8,15},{9,8},{10,9... | collective-permute-start | bytes 1179656 | tf_op jit(solution)/shard_map/ppermute | solution.py:799
  (50 other events, 978.8 us)
Sparse Core Ops, SparseCore 0:
  98.2 43.7 all-reduce.2
  190.6 36.3 all-reduce.4

commit v2 on v1

--- a/solution.py
+++ b/solution.py
@@ -388,7 +388,7 @@
 
     used = [0] if groups == 1 else [0, 1 + (2 * i > last).astype(jnp.int32)]
     for group in used:
-        places = ones_at(codes[group] - i * near * size_y, near * size_y, 1)
+        places = ones_at(codes[group][:, :1] - i * near * size_y, near * size_y, 1)
         gathered[group] += jnp.dot(places, result, preferred_element_type=jnp.float32)
 
     @pl.when(i == last)
@@ -741,8 +741,12 @@
     found = [codes_of(outer, shift) for shift in (0, -1, 1)]
     codes_outer, sides_outer = (jnp.stack(values) for values in zip(*found))
     codes_inner, sides_inner = (values[None] for values in codes_of(inner, 0))
-    sides_outer, sides_inner = sides_outer[:, :, None], sides_inner[:, :, None]
-    rows_codes = [codes_outer[:, :, None], codes_inner[:, :, None]]
+
+    def on_lanes(values):
+        return jnp.broadcast_to(values[:, :, None], (*values.shape, cells))
+
+    sides_outer, sides_inner = on_lanes(sides_outer), on_lanes(sides_inner)
+    rows_codes = [on_lanes(codes_outer), on_lanes(codes_inner)]
     lane_codes = [codes_outer[:, None, :], codes_inner[:, None, :]]
     strength = 3.0 * math.sqrt(cells * blocks) / nproj
     coupled = (coupling + coupling.T) * (0.5 * strength)

time: 272 us -> 275 us (1.011)
  waiting for transfers between devices: 134 us -> 139 us
    optimization_barrier x4 -> x0, local copies, waits for them, and re-layouts: 3.49 us -> none  [per_device_chunked(): lax.optimization_barrier((section_inner, rows_codes, lane_codes, sides_ou...]
    broadcast_in_dim x0 -> x6, local copies, waits for them, and re-layouts: none -> 3.47 us  [on_lanes(): return jnp.broadcast_to(values[:, :, None], (*values.shape, cells))]
    ppermute x14, waiting for transfers between devices: 63.1 us -> 66 us  [permute_all(): received.append(lax.ppermute(block, 'fft', pairs))]
  transfers between devices with their start and end apart: 34 -> 34, of which waited for: 16 -> 14; matrix products, arithmetic and copies ran while one was open for 5% -> 5% of each run, Pallas kernels for 14% -> 14%
where the time goes in v2:
time: 275 us
  waiting for transfers between devices  139 us (51%)
  Pallas kernels  53.2 us (19%)
  starting transfers between devices  53.1 us (19%)
  between operations  14.4 us (5%)
  local copies, waits for them, and re-layouts  12.1 us (4%)
  other arithmetic  3.6 us (1%)
    ppermute x14, waiting for transfers between devices, send(): return lax.ppermute(block, 'fft', [(j, j ^ k) for j in range(pieces)])  69.5 us
    ppermute x14, waiting for transfers between devices, permute_all(): received.append(lax.ppermute(block, 'fft', pairs))  66 us
    ppermute x14, starting transfers between devices, permute_all(): received.append(lax.ppermute(block, 'fft', pairs))  29.3 us
    ppermute x14, starting transfers between devices, send(): return lax.ppermute(block, 'fft', [(j, j ^ k) for j in range(pieces)])  17.8 us
    pallas_call x2, Pallas kernels, make_field(): pl.pallas_call(functools.partial(field_kernel, pieces=pieces, count=len(b...  15.3 us
    pallas_call x2, Pallas kernels, go_back(): pl.pallas_call(functools.partial(back_kernel, pieces=pieces, natural=natu...  15 us
    pallas_call x2, Pallas kernels, first_x(): pl.pallas_call(functools.partial(first_x_kernel, pieces=pieces, natural=n...  11.7 us
    pallas_call x1, Pallas kernels, last_x(): pl.pallas_call(last_x_kernel, grid=(2,), in_specs=[SMEM_SPEC, pl.BlockSpe...  8.93 us
  transfers between devices with their start and end apart: 34, of which 14 were waited for; matrix products, arithmetic and copies ran while one was open for 5% of the time, Pallas kernels for 14%

profile of v2, /device:TPU:10, one launch (start us, length us, event | category | flops | bytes accessed | tf_op | source)
XLA Modules:
  0.0 275.0 jit_solution(13875042586732028279)
XLA Ops:
  7.2 6.3 %first_x.2 = (bf16[24,32,256]{2,1,0:T(8,128)(2,1)}, bf16[24,32,256]{2,1,0:T(8,128)(2,1)}, bf16[24,32,256]{2,1,0:T(8,128)(2,1)}, bf16[24,32,256]{2,1,0:T(8,128)(2...) custom-call(s32[1]{0:T(128)} %bitcast.2.slab, ...), custom_call_target="tpu_custom_call" | custom-call | flops 1207959552 | bytes 9437184 | tf_op jit(solution)/shard_map/first_x/pallas_call | solution.py:274
  18.6 6.1 %collective-permute-done.refs_1_ = bf16[24,32,256]{2,1,0:T(8,128)(2,1)S(1)} collective-permute-done((bf16[24,32,256]{2,1,0:T(8,128)(2,1)}, bf16[24,32,256]{2,1,0:T(8,128)(2,1)S(1)}, u32[]{:S(2)}, u32[]{:S(2)}) %collective-permute-start) | collective-permute-done | bytes 393248 | tf_op jit(solution)/shard_map/ppermute | solution.py:766
  24.8 17.2 %collective-permute-done.3.refs_4_ = bf16[24,32,256]{2,1,0:T(8,128)(2,1)S(1)} collective-permute-done((bf16[24,32,256]{2,1,0:T(8,128)(2,1)}, bf16[24,32,256]{2,1,0:T(8,128)(2,1)S(1)}, u32[]{:S(2)}, u32[]{:S(2)}) %collective-permute-start.3) | collective-permute-done | bytes 393248 | tf_op jit(solution)/shard_map/ppermute | solution.py:766
  42.4 9.2 %collective-permute-done.4.refs_5_ = bf16[24,32,256]{2,1,0:T(8,128)(2,1)S(1)} collective-permute-done((bf16[24,32,256]{2,1,0:T(8,128)(2,1)}, bf16[24,32,256]{2,1,0:T(8,128)(2,1)S(1)}, u32[]{:S(2)}, u32[]{:S(2)}) %collective-permute-start.4) | collective-permute-done | bytes 393248 | tf_op jit(solution)/shard_map/ppermute | solution.py:766
  54.9 5.3 %first_x.3 = (bf16[24,16,256]{2,1,0:T(8,128)(2,1)}, bf16[24,16,256]{2,1,0:T(8,128)(2,1)}, bf16[24,16,256]{2,1,0:T(8,128)(2,1)}, bf16[24,16,256]{2,1,0:T(8,128)(2...) custom-call(s32[1]{0:T(128)} %bitcast.2.slab, ...), custom_call_target="tpu_custom_call" | custom-call | flops 603979776 | bytes 9437184 | tf_op jit(solution)/shard_map/first_x/pallas_call | solution.py:274
  64.8 11.7 %collective-permute-done.5.refs_6_ = bf16[24,32,256]{2,1,0:T(8,128)(2,1)S(1)} collective-permute-done((bf16[24,32,256]{2,1,0:T(8,128)(2,1)}, bf16[24,32,256]{2,1,0:T(8,128)(2,1)S(1)}, u32[]{:S(2)}, u32[]{:S(2)}) %collective-permute-start.5) | collective-permute-done | bytes 393248 | tf_op jit(solution)/shard_map/ppermute | solution.py:766
  76.5 8.3 %collective-permute-done.6.refs_7_ = bf16[24,32,256]{2,1,0:T(8,128)(2,1)S(1)} collective-permute-done((bf16[24,32,256]{2,1,0:T(8,128)(2,1)}, bf16[24,32,256]{2,1,0:T(8,128)(2,1)S(1)}, u32[]{:S(2)}, u32[]{:S(2)}) %collective-permute-start.6) | collective-permute-done | bytes 393248 | tf_op jit(solution)/shard_map/ppermute | solution.py:766
  84.8 3.1 %collective-permute-start.10 = (bf16[24,16,256]{2,1,0:T(8,128)(2,1)}, bf16[24,16,256]{2,1,0:T(8,128)(2,1)S(1)}, u32[]{:S(2)}, u32[]{:S(2)}) collective-permute-start(bf16[24,16,256]{2,1,0:T(8,128)(2,1)} %get-tuple-element.166), channel_id=1, source_target_pairs={{0,4},{1,5},{2,6},{3,7},{4,0},{5,1},{6,2},{7,3},{8,12},{9,13},{10,... | collective-permute-start | bytes 589832 | tf_op jit(solution)/shard_map/ppermute | solution.py:766
  87.9 9.8 %make_field.2 = (bf16[2,16,192,256]{3,2,1,0:T(8,128)(2,1)}, bf16[16,192,256]{2,1,0:T(8,128)(2,1)}, bf16[2,256,128]{2,1,0:T(8,128)(2,1)}, bf16[2,256,128]{2,1,0:T(8,128)(2,1)}, bf16[2,256,128]{2,1,0:T(8,128)(2,1)}) custom-call(s32[1]{0:T(128)} %bitcast.2.slab, f32[1,2]{1,0:T(1,128)} %weights.3, bf16[2,192,192]{2,1,0:T(8,128)(2,1)} %constant.172.clone.table_y, ...), custom_call_target="tpu_custom_call" | custom-call | flops 2818572288 | bytes 6291456 | tf_op jit(solution)/shard_map/make_field/pallas_call | solution.py:418
  111.0 12.9 %collective-permute-done.8.refs_2_ = bf16[24,16,256]{2,1,0:T(8,128)(2,1)S(1)} collective-permute-done((bf16[24,16,256]{2,1,0:T(8,128)(2,1)S(1)}, bf16[24,16,256]{2,1,0:T(8,128)(2,1)S(1)}, u32[]{:S(2)}, u32[]{:S(2)}) %collective-permute-start.8) | collective-permute-done | bytes 196640 | tf_op jit(solution)/shard_map/ppermute | solution.py:766
  126.1 5.5 %make_field.3 = (bf16[2,8,192,256]{3,2,1,0:T(8,128)(2,1)}, bf16[8,192,256]{2,1,0:T(8,128)(2,1)}, bf16[2,256,128]{2,1,0:T(8,128)(2,1)}) custom-call(s32[1]{0:T(128)} %bitcast.2.slab, f32[1,2]{1,0:T(1,128)} %weights.3, bf16[2,192,192]{2,1,0:T(8,128)(2,1)} %constant.172.clone.table_y, bf16[512,512]{1,0:T(8,128)(2,1)} %constant.173.clone.table_z, ...), custom_call_target="tpu_custom_call" | custom-call | flops 1409286144 | bytes 3145728 | tf_op jit(solution)/shard_map/make_field/pallas_call | solution.py:418
  134.7 2.9 %collective-permute-start.16 = (bf16[2,256,128]{2,1,0:T(8,128)(2,1)}, bf16[2,256,128]{2,1,0:T(8,128)(2,1)S(1)}, u32[]{:S(2)}, u32[]{:S(2)}) collective-permute-start(bf16[2,256,128]{2,1,0:T(8,128)(2,1)} %get-tuple-element.176.refs_0_), channel_id=1, source_target_pairs={{0,1},{1,2},{2,3},{3,4},{4,5},{5,6},{6,7},{7,0},{8,9},{9,10},{10,1... | collective-permute-start | bytes 393224 | tf_op jit(solution)/shard_map/ppermute | solution.py:791
  137.6 5.4 %go_back.3 = (bf16[24,16,256]{2,1,0:T(8,128)(2,1)}, bf16[24,16,256]{2,1,0:T(8,128)(2,1)}, bf16[24,16,256]{2,1,0:T(8,128)(2,1)}, bf16[24,16,256]{2,1,0:T(8,128)(2...) custom-call(s32[1]{0:T(128)} %bitcast.2.slab, ...), custom_call_target="tpu_custom_call" | custom-call | flops 1409286144 | bytes 3145728 | tf_op jit(solution)/shard_map/go_back/pallas_call | solution.py:578
  146.0 3.2 %collective-permute-start.21 = (bf16[24,16,256]{2,1,0:T(8,128)(2,1)}, bf16[24,16,256]{2,1,0:T(8,128)(2,1)S(1)}, u32[]{:S(2)}, u32[]{:S(2)}) collective-permute-start(bf16[24,16,256]{2,1,0:T(8,128)(2,1)} %get-tuple-element.196), channel_id=1, source_target_pairs={{0,2},{1,3},{2,4},{3,5},{4,6},{5,7},{6,0},{7,1},{8,10},{9,11},{10,... | collective-permute-start | bytes 589832 | tf_op jit(solution)/shard_map/ppermute | solution.py:803
  149.9 9.5 %go_back.2 = (bf16[24,32,256]{2,1,0:T(8,128)(2,1)}, bf16[24,32,256]{2,1,0:T(8,128)(2,1)}, bf16[24,32,256]{2,1,0:T(8,128)(2,1)}, bf16[24,32,256]{2,1,0:T(8,128)(2...) custom-call(s32[1]{0:T(128)} %bitcast.2.slab, ...), custom_call_target="tpu_custom_call" | custom-call | flops 2818572288 | bytes 6291456 | tf_op jit(solution)/shard_map/go_back/pallas_call | solution.py:578
  159.4 2.8 %collective-permute-start.25 = (bf16[24,32,256]{2,1,0:T(8,128)(2,1)}, bf16[24,32,256]{2,1,0:T(8,128)(2,1)S(1)}, u32[]{:S(2)}, u32[]{:S(2)}) collective-permute-start(bf16[24,32,256]{2,1,0:T(8,128)(2,1)} %get-tuple-element.202), channel_id=1, source_target_pairs={{0,4},{1,5},{2,6},{3,7},{4,0},{5,1},{6,2},{7,3},{8,12},{9,13},{10,... | collective-permute-start | bytes 1179656 | tf_op jit(solution)/shard_map/ppermute | solution.py:803
  163.0 11.0 %collective-permute-done.19.refs_10_ = bf16[24,16,256]{2,1,0:T(8,128)(2,1)S(1)} collective-permute-done((bf16[24,16,256]{2,1,0:T(8,128)(2,1)}, bf16[24,16,256]{2,1,0:T(8,128)(2,1)S(1)}, u32[]{:S(2)}, u32[]{:S(2)}) %collective-permute-start.19) | collective-permute-done | bytes 196640 | tf_op jit(solution)/shard_map/ppermute | solution.py:803
  174.0 12.2 %collective-permute-start.22 = (bf16[24,16,256]{2,1,0:T(8,128)(2,1)S(1)}, bf16[24,16,256]{2,1,0:T(8,128)(2,1)S(1)}, u32[]{:S(2)}, u32[]{:S(2)}) collective-permute-start(bf16[24,16,256]{2,1,0:T(8,128)(2,1)S(1)} %copy-done.31), channel_id=1, source_target_pairs={{0,6},{1,7},{2,0},{3,1},{4,2},{5,3},{6,4},{7,5},{8,14},{9,15},{10,... | collective-permute-start | bytes 589832 | tf_op jit(solution)/shard_map/ppermute | solution.py:803
  192.2 25.4 %collective-permute-done.22.refs_13_ = bf16[24,16,256]{2,1,0:T(8,128)(2,1)S(1)} collective-permute-done((bf16[24,16,256]{2,1,0:T(8,128)(2,1)S(1)}, bf16[24,16,256]{2,1,0:T(8,128)(2,1)S(1)}, u32[]{:S(2)}, u32[]{:S(2)}) %collective-permute-start.22) | collective-permute-done | bytes 196640 | tf_op jit(solution)/shard_map/ppermute | solution.py:803
  223.9 3.0 %all-reduce.5.cloned.1.call-done = bf16[8,192,256]{2,1,0:T(8,128)(2,1)} async-done(((bf16[8,192,256]{2,1,0:T(8,128)(2,1)}), bf16[8,192,256]{2,1,0:T(8,128)(2,1)}) %all-reduce.5.cloned.1.call-update) | async-done | bytes 786448 | tf_op jit(solution)/shard_map/psum | solution.py:813
  229.6 6.2 %collective-permute-done.27.refs_3_ = bf16[24,32,256]{2,1,0:T(8,128)(2,1)S(1)} collective-permute-done((bf16[24,32,256]{2,1,0:T(8,128)(2,1)}, bf16[24,32,256]{2,1,0:T(8,128)(2,1)S(1)}, u32[]{:S(2)}, u32[]{:S(2)}) %collective-permute-start.27) | collective-permute-done | bytes 393248 | tf_op jit(solution)/shard_map/ppermute | solution.py:803
  235.8 12.1 %collective-permute-done.29.refs_5_ = bf16[24,32,256]{2,1,0:T(8,128)(2,1)S(1)} collective-permute-done((bf16[24,32,256]{2,1,0:T(8,128)(2,1)}, bf16[24,32,256]{2,1,0:T(8,128)(2,1)S(1)}, u32[]{:S(2)}, u32[]{:S(2)}) %collective-permute-start.29) | collective-permute-done | bytes 393248 | tf_op jit(solution)/shard_map/ppermute | solution.py:803
  247.9 11.3 %collective-permute-done.31.refs_7_ = bf16[24,32,256]{2,1,0:T(8,128)(2,1)} collective-permute-done((bf16[24,32,256]{2,1,0:T(8,128)(2,1)}, bf16[24,32,256]{2,1,0:T(8,128)(2,1)}, u32[]{:S(2)}, u32[]{:S(2)}) %collective-permute-start.31) | collective-permute-done | bytes 393248 | tf_op jit(solution)/shard_map/ppermute | solution.py:803
  259.2 8.9 %last_x.1 = bf16[2,192,24,256]{3,2,1,0:T(8,128)(2,1)} custom-call(f32[192]{0:T(256)} %constant.177.clone.frequency_x, f32[24,256]{1,0:T(8,128)} %broadcast_add_fusion.frequency_yz, bf16[384,384]{1,0:T(8,128)(2,1)} %dynamic-slice_bitcast_fusion.table, bf16[2,192,24,256]{3,2,1,0:T(8,128)(2,1)} %bitcast.16, bf16[24,32,256]{2,1,0:T(8,128)(2,1)} %get-tuple-element.201.refs_0_, ...), custom_call_target="tpu_custom_call" | custom-call | flops 1811939328 | bytes 14155776 | tf_op jit(solution)/shard_map/last_x/pallas_call | solution.py:636
  (163 shorter events, 51.1 us)
Async XLA Ops:
  7.2 152.3 %all-reduce.3.cloned.1.call-start = ((), (), s32[]{:S(2)}) async-start(), calls=%async_computation | async-start | bytes 3145728 | tf_op jit(solution)/shard_map/psum | solution.py:783
  14.1 27.9 %collective-permute-start.3 = (bf16[24,32,256]{2,1,0:T(8,128)(2,1)}, bf16[24,32,256]{2,1,0:T(8,128)(2,1)S(1)}, u32[]{:S(2)}, u32[]{:S(2)}) collective-permute-start(bf16[24,32,256]{2,1,0:T(8,128)(2,1)} %get-tuple-element.142), channel_id=1, source_target_pairs={{0,4},{1,5},{2,6},{3,7},{4,0},{5,1},{6,2},{7,3},{8,12},{9,13},{10,... | collective-permute-start | bytes 1179656 | tf_op jit(solution)/shard_map/ppermute | solution.py:766
  16.7 34.9 %collective-permute-start.4 = (bf16[24,32,256]{2,1,0:T(8,128)(2,1)}, bf16[24,32,256]{2,1,0:T(8,128)(2,1)S(1)}, u32[]{:S(2)}, u32[]{:S(2)}) collective-permute-start(bf16[24,32,256]{2,1,0:T(8,128)(2,1)} %get-tuple-element.145), channel_id=1, source_target_pairs={{0,5},{1,4},{2,7},{3,6},{4,1},{5,0},{6,3},{7,2},{8,13},{9,12},{10,... | collective-permute-start | bytes 1179656 | tf_op jit(solution)/shard_map/ppermute | solution.py:766
  18.0 46.3 %collective-permute-start.1 = (bf16[24,32,256]{2,1,0:T(8,128)(2,1)}, bf16[24,32,256]{2,1,0:T(8,128)(2,1)S(1)}, u32[]{:S(2)}, u32[]{:S(2)}) collective-permute-start(bf16[24,32,256]{2,1,0:T(8,128)(2,1)} %get-tuple-element.136), channel_id=1, source_target_pairs={{0,2},{1,3},{2,0},{3,1},{4,6},{5,7},{6,4},{7,5},{8,10},{9,11},{10,... | collective-permute-start | bytes 1179656 | tf_op jit(solution)/shard_map/ppermute | solution.py:766
  24.7 40.1 %collective-permute-start.2 = (bf16[24,32,256]{2,1,0:T(8,128)(2,1)}, bf16[24,32,256]{2,1,0:T(8,128)(2,1)S(1)}, u32[]{:S(2)}, u32[]{:S(2)}) collective-permute-start(bf16[24,32,256]{2,1,0:T(8,128)(2,1)} %get-tuple-element.139), channel_id=1, source_target_pairs={{0,3},{1,2},{2,1},{3,0},{4,7},{5,6},{6,5},{7,4},{8,11},{9,10},{10,... | collective-permute-start | bytes 1179656 | tf_op jit(solution)/shard_map/ppermute | solution.py:766
  42.0 34.5 %collective-permute-start.5 = (bf16[24,32,256]{2,1,0:T(8,128)(2,1)}, bf16[24,32,256]{2,1,0:T(8,128)(2,1)S(1)}, u32[]{:S(2)}, u32[]{:S(2)}) collective-permute-start(bf16[24,32,256]{2,1,0:T(8,128)(2,1)} %get-tuple-element.148), channel_id=1, source_target_pairs={{0,6},{1,7},{2,4},{3,5},{4,2},{5,3},{6,0},{7,1},{8,14},{9,15},{10,... | collective-permute-start | bytes 1179656 | tf_op jit(solution)/shard_map/ppermute | solution.py:766
  51.7 33.1 %collective-permute-start.6 = (bf16[24,32,256]{2,1,0:T(8,128)(2,1)}, bf16[24,32,256]{2,1,0:T(8,128)(2,1)S(1)}, u32[]{:S(2)}, u32[]{:S(2)}) collective-permute-start(bf16[24,32,256]{2,1,0:T(8,128)(2,1)} %get-tuple-element.151), channel_id=1, source_target_pairs={{0,7},{1,6},{2,5},{3,4},{4,3},{5,2},{6,1},{7,0},{8,15},{9,14},{10,... | collective-permute-start | bytes 1179656 | tf_op jit(solution)/shard_map/ppermute | solution.py:766
  64.3 33.4 %collective-permute-start.7 = (bf16[24,16,256]{2,1,0:T(8,128)(2,1)}, bf16[24,16,256]{2,1,0:T(8,128)(2,1)S(1)}, u32[]{:S(2)}, u32[]{:S(2)}) collective-permute-start(bf16[24,16,256]{2,1,0:T(8,128)(2,1)} %get-tuple-element.161), channel_id=1, source_target_pairs={{0,1},{1,0},{2,3},{3,2},{4,5},{5,4},{6,7},{7,6},{8,9},{9,8},{10,11... | collective-permute-start | bytes 589832 | tf_op jit(solution)/shard_map/ppermute | solution.py:766
  97.7 129.2 %all-reduce.5.cloned.1.call-start = ((), (), s32[]{:S(2)}) async-start(), calls=%async_computation.1 | async-start | bytes 1572864 | tf_op jit(solution)/shard_map/psum | solution.py:813
  99.7 24.3 %collective-permute-start.8 = (bf16[24,16,256]{2,1,0:T(8,128)(2,1)S(1)}, bf16[24,16,256]{2,1,0:T(8,128)(2,1)S(1)}, u32[]{:S(2)}, u32[]{:S(2)}) collective-permute-start(bf16[24,16,256]{2,1,0:T(8,128)(2,1)S(1)} %copy-done.27), channel_id=1, source_target_pairs={{0,2},{1,3},{2,0},{3,1},{4,6},{5,7},{6,4},{7,5},{8,10},{9,11},{10,... | collective-permute-start | bytes 589832 | tf_op jit(solution)/shard_map/ppermute | solution.py:766
  100.6 23.4 %collective-permute-start.13 = (bf16[24,16,256]{2,1,0:T(8,128)(2,1)S(1)}, bf16[24,16,256]{2,1,0:T(8,128)(2,1)S(1)}, u32[]{:S(2)}, u32[]{:S(2)}) collective-permute-start(bf16[24,16,256]{2,1,0:T(8,128)(2,1)S(1)} %copy-done.25), channel_id=1, source_target_pairs={{0,7},{1,6},{2,5},{3,4},{4,3},{5,2},{6,1},{7,0},{8,15},{9,14},{10,... | collective-permute-start | bytes 589832 | tf_op jit(solution)/shard_map/ppermute | solution.py:766
  105.3 26.4 %collective-permute-start.14 = (bf16[2,256,128]{2,1,0:T(8,128)(2,1)}, bf16[2,256,128]{2,1,0:T(8,128)(2,1)S(1)}, u32[]{:S(2)}, u32[]{:S(2)}) collective-permute-start(bf16[2,256,128]{2,1,0:T(8,128)(2,1)} %get-tuple-element.174), channel_id=1, source_target_pairs={{1,0},{2,1},{3,2},{4,3},{5,4},{6,5},{7,6},{0,7},{9,8},{10,9},{11,1... | collective-permute-start | bytes 393224 | tf_op jit(solution)/shard_map/ppermute | solution.py:781
  108.6 23.1 %collective-permute-start.15 = (bf16[2,256,128]{2,1,0:T(8,128)(2,1)}, bf16[2,256,128]{2,1,0:T(8,128)(2,1)S(1)}, u32[]{:S(2)}, u32[]{:S(2)}) collective-permute-start(bf16[2,256,128]{2,1,0:T(8,128)(2,1)} %get-tuple-element.175), channel_id=1, source_target_pairs={{0,1},{1,2},{2,3},{3,4},{4,5},{5,6},{6,7},{7,0},{8,9},{9,10},{10,1... | collective-permute-start | bytes 393224 | tf_op jit(solution)/shard_map/ppermute | solution.py:782
  143.1 30.9 %collective-permute-start.19 = (bf16[24,16,256]{2,1,0:T(8,128)(2,1)}, bf16[24,16,256]{2,1,0:T(8,128)(2,1)S(1)}, u32[]{:S(2)}, u32[]{:S(2)}) collective-permute-start(bf16[24,16,256]{2,1,0:T(8,128)(2,1)} %get-tuple-element.194), channel_id=1, source_target_pairs={{0,3},{1,4},{2,5},{3,6},{4,7},{5,0},{6,1},{7,2},{8,11},{9,12},{10,... | collective-permute-start | bytes 589832 | tf_op jit(solution)/shard_map/ppermute | solution.py:803
  145.8 40.4 %collective-permute-start.20 = (bf16[24,16,256]{2,1,0:T(8,128)(2,1)}, bf16[24,16,256]{2,1,0:T(8,128)(2,1)S(1)}, u32[]{:S(2)}, u32[]{:S(2)}) collective-permute-start(bf16[24,16,256]{2,1,0:T(8,128)(2,1)} %get-tuple-element.195), channel_id=1, source_target_pairs={{0,5},{1,6},{2,7},{3,0},{4,1},{5,2},{6,3},{7,4},{8,13},{9,14},{10,... | collective-permute-start | bytes 589832 | tf_op jit(solution)/shard_map/ppermute | solution.py:803
  146.0 42.2 %collective-permute-start.21 = (bf16[24,16,256]{2,1,0:T(8,128)(2,1)}, bf16[24,16,256]{2,1,0:T(8,128)(2,1)S(1)}, u32[]{:S(2)}, u32[]{:S(2)}) collective-permute-start(bf16[24,16,256]{2,1,0:T(8,128)(2,1)} %get-tuple-element.196), channel_id=1, source_target_pairs={{0,2},{1,3},{2,4},{3,5},{4,6},{5,7},{6,0},{7,1},{8,10},{9,11},{10,... | collective-permute-start | bytes 589832 | tf_op jit(solution)/shard_map/ppermute | solution.py:803
  159.4 60.4 %collective-permute-start.25 = (bf16[24,32,256]{2,1,0:T(8,128)(2,1)}, bf16[24,32,256]{2,1,0:T(8,128)(2,1)S(1)}, u32[]{:S(2)}, u32[]{:S(2)}) collective-permute-start(bf16[24,32,256]{2,1,0:T(8,128)(2,1)} %get-tuple-element.202), channel_id=1, source_target_pairs={{0,4},{1,5},{2,6},{3,7},{4,0},{5,1},{6,2},{7,3},{8,12},{9,13},{10,... | collective-permute-start | bytes 1179656 | tf_op jit(solution)/shard_map/ppermute | solution.py:803
  162.3 59.9 %collective-permute-start.26 = (bf16[24,32,256]{2,1,0:T(8,128)(2,1)}, bf16[24,32,256]{2,1,0:T(8,128)(2,1)S(1)}, u32[]{:S(2)}, u32[]{:S(2)}) collective-permute-start(bf16[24,32,256]{2,1,0:T(8,128)(2,1)} %get-tuple-element.203), channel_id=1, source_target_pairs={{0,3},{1,4},{2,5},{3,6},{4,7},{5,0},{6,1},{7,2},{8,11},{9,12},{10,... | collective-permute-start | bytes 1179656 | tf_op jit(solution)/shard_map/ppermute | solution.py:803
  174.0 43.7 %collective-permute-start.22 = (bf16[24,16,256]{2,1,0:T(8,128)(2,1)S(1)}, bf16[24,16,256]{2,1,0:T(8,128)(2,1)S(1)}, u32[]{:S(2)}, u32[]{:S(2)}) collective-permute-start(bf16[24,16,256]{2,1,0:T(8,128)(2,1)S(1)} %copy-done.31), channel_id=1, source_target_pairs={{0,6},{1,7},{2,0},{3,1},{4,2},{5,3},{6,4},{7,5},{8,14},{9,15},{10,... | collective-permute-start | bytes 589832 | tf_op jit(solution)/shard_map/ppermute | solution.py:803
  186.2 31.5 %collective-permute-start.23 = (bf16[24,16,256]{2,1,0:T(8,128)(2,1)S(1)}, bf16[24,16,256]{2,1,0:T(8,128)(2,1)S(1)}, u32[]{:S(2)}, u32[]{:S(2)}) collective-permute-start(bf16[24,16,256]{2,1,0:T(8,128)(2,1)S(1)} %copy-done.28), channel_id=1, source_target_pairs={{0,1},{1,2},{2,3},{3,4},{4,5},{5,6},{6,7},{7,0},{8,9},{9,10},{10,1... | collective-permute-start | bytes 589832 | tf_op jit(solution)/shard_map/ppermute | solution.py:803
  188.2 29.6 %collective-permute-start.24 = (bf16[24,16,256]{2,1,0:T(8,128)(2,1)S(1)}, bf16[24,16,256]{2,1,0:T(8,128)(2,1)S(1)}, u32[]{:S(2)}, u32[]{:S(2)}) collective-permute-start(bf16[24,16,256]{2,1,0:T(8,128)(2,1)S(1)} %copy-done.26), channel_id=1, source_target_pairs={{0,7},{1,0},{2,1},{3,2},{4,3},{5,4},{6,5},{7,6},{8,15},{9,8},{10,9... | collective-permute-start | bytes 589832 | tf_op jit(solution)/shard_map/ppermute | solution.py:803
  217.8 30.1 %collective-permute-start.29 = (bf16[24,32,256]{2,1,0:T(8,128)(2,1)}, bf16[24,32,256]{2,1,0:T(8,128)(2,1)S(1)}, u32[]{:S(2)}, u32[]{:S(2)}) collective-permute-start(bf16[24,32,256]{2,1,0:T(8,128)(2,1)} %get-tuple-element.206), channel_id=1, source_target_pairs={{0,6},{1,7},{2,0},{3,1},{4,2},{5,3},{6,4},{7,5},{8,14},{9,15},{10,... | collective-permute-start | bytes 1179656 | tf_op jit(solution)/shard_map/ppermute | solution.py:803
  219.8 28.1 %collective-permute-start.30 = (bf16[24,32,256]{2,1,0:T(8,128)(2,1)}, bf16[24,32,256]{2,1,0:T(8,128)(2,1)}, u32[]{:S(2)}, u32[]{:S(2)}) collective-permute-start(bf16[24,32,256]{2,1,0:T(8,128)(2,1)} %get-tuple-element.207), channel_id=1, source_target_pairs={{0,1},{1,2},{2,3},{3,4},{4,5},{5,6},{6,7},{7,0},{8,9},{9,10},{10,1... | collective-permute-start | bytes 1179656 | tf_op jit(solution)/shard_map/ppermute | solution.py:803
  222.2 37.0 %collective-permute-start.31 = (bf16[24,32,256]{2,1,0:T(8,128)(2,1)}, bf16[24,32,256]{2,1,0:T(8,128)(2,1)}, u32[]{:S(2)}, u32[]{:S(2)}) collective-permute-start(bf16[24,32,256]{2,1,0:T(8,128)(2,1)} %get-tuple-element.208), channel_id=1, source_target_pairs={{0,7},{1,0},{2,1},{3,2},{4,3},{5,4},{6,5},{7,6},{8,15},{9,8},{10,9... | collective-permute-start | bytes 1179656 | tf_op jit(solution)/shard_map/ppermute | solution.py:803
  (50 other events, 957.5 us)
Sparse Core Ops, SparseCore 0:
  97.8 43.7 all-reduce.2
  191.7 35.1 all-reduce.4

commit v3 on v1

--- a/solution.py
+++ b/solution.py
@@ -14,7 +14,7 @@
 PLANES = 4
 COLUMNS = 8
 FOUR = 4
-VMEM_BYTES = 56 * 1024 * 1024
+VMEM_BYTES = 61 * 1024 * 1024
 
 
 def extended(shard, sides, width):

time: 272 us -> 268 us (0.985); the launches traced: 271 us -> 265 us
  waiting for transfers between devices: 134 us -> 124 us
    ppermute x14, waiting for transfers between devices: 63.1 us -> 54.1 us  [permute_all(): received.append(lax.ppermute(block, 'fft', pairs))]
  transfers between devices with their start and end apart: 34 -> 34, of which waited for: 16 -> 15; matrix products, arithmetic and copies ran while one was open for 5% -> 5% of each run, Pallas kernels for 14% -> 15%
where the time goes in v3:
time: 268 us; the launch traced here: 265 us
  waiting for transfers between devices  124 us (46%)
  starting transfers between devices  55.7 us (21%)
  Pallas kernels  54.1 us (20%)
  between operations  14.4 us (5%)
  local copies, waits for them, and re-layouts  12.9 us (5%)
  other arithmetic  3.58 us (1%)
    ppermute x14, waiting for transfers between devices, send(): return lax.ppermute(block, 'fft', [(j, j ^ k) for j in range(pieces)])  68.9 us
    ppermute x14, waiting for transfers between devices, permute_all(): received.append(lax.ppermute(block, 'fft', pairs))  54.1 us
    ppermute x14, starting transfers between devices, permute_all(): received.append(lax.ppermute(block, 'fft', pairs))  31.7 us
    ppermute x14, starting transfers between devices, send(): return lax.ppermute(block, 'fft', [(j, j ^ k) for j in range(pieces)])  15.9 us
    pallas_call x2, Pallas kernels, make_field(): pl.pallas_call(functools.partial(field_kernel, pieces=pieces, count=len(b...  15.8 us
    pallas_call x2, Pallas kernels, go_back(): pl.pallas_call(functools.partial(back_kernel, pieces=pieces, natural=natu...  15.4 us
    pallas_call x2, Pallas kernels, first_x(): pl.pallas_call(functools.partial(first_x_kernel, pieces=pieces, natural=n...  11.7 us
    pallas_call x1, Pallas kernels, last_x(): pl.pallas_call(last_x_kernel, grid=(2,), in_specs=[SMEM_SPEC, pl.BlockSpe...  8.93 us
  transfers between devices with their start and end apart: 34, of which 15 were waited for; matrix products, arithmetic and copies ran while one was open for 5% of the time, Pallas kernels for 15%

profile of v3, /device:TPU:10, one launch (start us, length us, event | category | flops | bytes accessed | tf_op | source)
XLA Modules:
  0.0 264.7 jit_solution(17192768388776211984)
XLA Ops:
  7.2 6.3 %first_x.2 = (bf16[24,32,256]{2,1,0:T(8,128)(2,1)}, bf16[24,32,256]{2,1,0:T(8,128)(2,1)}, bf16[24,32,256]{2,1,0:T(8,128)(2,1)}, bf16[24,32,256]{2,1,0:T(8,128)(2...) custom-call(s32[1]{0:T(128)} %bitcast.2.slab, ...), custom_call_target="tpu_custom_call" | custom-call | flops 1207959552 | bytes 9437184 | tf_op jit(solution)/shard_map/first_x/pallas_call | solution.py:274
  18.6 6.1 %collective-permute-done.refs_1_ = bf16[24,32,256]{2,1,0:T(8,128)(2,1)S(1)} collective-permute-done((bf16[24,32,256]{2,1,0:T(8,128)(2,1)}, bf16[24,32,256]{2,1,0:T(8,128)(2,1)S(1)}, u32[]{:S(2)}, u32[]{:S(2)}) %collective-permute-start) | collective-permute-done | bytes 393248 | tf_op jit(solution)/shard_map/ppermute | solution.py:762
  24.8 17.2 %collective-permute-done.3.refs_4_ = bf16[24,32,256]{2,1,0:T(8,128)(2,1)S(1)} collective-permute-done((bf16[24,32,256]{2,1,0:T(8,128)(2,1)}, bf16[24,32,256]{2,1,0:T(8,128)(2,1)S(1)}, u32[]{:S(2)}, u32[]{:S(2)}) %collective-permute-start.3) | collective-permute-done | bytes 393248 | tf_op jit(solution)/shard_map/ppermute | solution.py:762
  42.4 9.2 %collective-permute-done.4.refs_5_ = bf16[24,32,256]{2,1,0:T(8,128)(2,1)S(1)} collective-permute-done((bf16[24,32,256]{2,1,0:T(8,128)(2,1)}, bf16[24,32,256]{2,1,0:T(8,128)(2,1)S(1)}, u32[]{:S(2)}, u32[]{:S(2)}) %collective-permute-start.4) | collective-permute-done | bytes 393248 | tf_op jit(solution)/shard_map/ppermute | solution.py:762
  54.9 5.3 %first_x.3 = (bf16[24,16,256]{2,1,0:T(8,128)(2,1)}, bf16[24,16,256]{2,1,0:T(8,128)(2,1)}, bf16[24,16,256]{2,1,0:T(8,128)(2,1)}, bf16[24,16,256]{2,1,0:T(8,128)(2...) custom-call(s32[1]{0:T(128)} %bitcast.2.slab, ...), custom_call_target="tpu_custom_call" | custom-call | flops 603979776 | bytes 9437184 | tf_op jit(solution)/shard_map/first_x/pallas_call | solution.py:274
  63.3 13.1 %collective-permute-done.5.refs_6_ = bf16[24,32,256]{2,1,0:T(8,128)(2,1)S(1)} collective-permute-done((bf16[24,32,256]{2,1,0:T(8,128)(2,1)}, bf16[24,32,256]{2,1,0:T(8,128)(2,1)S(1)}, u32[]{:S(2)}, u32[]{:S(2)}) %collective-permute-start.5) | collective-permute-done | bytes 393248 | tf_op jit(solution)/shard_map/ppermute | solution.py:762
  76.5 8.3 %collective-permute-done.6.refs_7_ = bf16[24,32,256]{2,1,0:T(8,128)(2,1)S(1)} collective-permute-done((bf16[24,32,256]{2,1,0:T(8,128)(2,1)}, bf16[24,32,256]{2,1,0:T(8,128)(2,1)S(1)}, u32[]{:S(2)}, u32[]{:S(2)}) %collective-permute-start.6) | collective-permute-done | bytes 393248 | tf_op jit(solution)/shard_map/ppermute | solution.py:762
  84.8 3.1 %collective-permute-start.10 = (bf16[24,16,256]{2,1,0:T(8,128)(2,1)}, bf16[24,16,256]{2,1,0:T(8,128)(2,1)S(1)}, u32[]{:S(2)}, u32[]{:S(2)}) collective-permute-start(bf16[24,16,256]{2,1,0:T(8,128)(2,1)} %get-tuple-element.166), channel_id=1, source_target_pairs={{0,4},{1,5},{2,6},{3,7},{4,0},{5,1},{6,2},{7,3},{8,12},{9,13},{10,... | collective-permute-start | bytes 589832 | tf_op jit(solution)/shard_map/ppermute | solution.py:762
  87.9 10.1 %make_field.2 = (bf16[2,16,192,256]{3,2,1,0:T(8,128)(2,1)}, bf16[16,192,256]{2,1,0:T(8,128)(2,1)}, bf16[2,256,128]{2,1,0:T(8,128)(2,1)}, bf16[2,256,128]{2,1,0:T(8,128)(2,1)}, bf16[2,256,128]{2,1,0:T(8,128)(2,1)}) custom-call(s32[1]{0:T(128)} %bitcast.2.slab, f32[1,2]{1,0:T(1,128)} %weights.3, bf16[2,192,192]{2,1,0:T(8,128)(2,1)} %constant.172.clone.table_y, ...), custom_call_target="tpu_custom_call" | custom-call | flops 2818572288 | bytes 6291456 | tf_op jit(solution)/shard_map/make_field/pallas_call | solution.py:418
  109.5 3.7 %collective-permute-start.15 = (bf16[2,256,128]{2,1,0:T(8,128)(2,1)}, bf16[2,256,128]{2,1,0:T(8,128)(2,1)S(1)}, u32[]{:S(2)}, u32[]{:S(2)}) collective-permute-start(bf16[2,256,128]{2,1,0:T(8,128)(2,1)} %get-tuple-element.175), channel_id=1, source_target_pairs={{0,1},{1,2},{2,3},{3,4},{4,5},{5,6},{6,7},{7,0},{8,9},{9,10},{10,1... | collective-permute-start | bytes 393224 | tf_op jit(solution)/shard_map/ppermute | solution.py:778
  114.3 3.8 %collective-permute-done.13.refs_7_ = bf16[24,16,256]{2,1,0:T(8,128)(2,1)S(1)} collective-permute-done((bf16[24,16,256]{2,1,0:T(8,128)(2,1)S(1)}, bf16[24,16,256]{2,1,0:T(8,128)(2,1)S(1)}, u32[]{:S(2)}, u32[]{:S(2)}) %collective-permute-start.13) | collective-permute-done | bytes 196640 | tf_op jit(solution)/shard_map/ppermute | solution.py:762
  118.1 7.9 %collective-permute-done.12.refs_6_ = bf16[24,16,256]{2,1,0:T(8,128)(2,1)S(1)} collective-permute-done((bf16[24,16,256]{2,1,0:T(8,128)(2,1)S(1)}, bf16[24,16,256]{2,1,0:T(8,128)(2,1)S(1)}, u32[]{:S(2)}, u32[]{:S(2)}) %collective-permute-start.12) | collective-permute-done | bytes 196640 | tf_op jit(solution)/shard_map/ppermute | solution.py:762
  126.7 5.7 %make_field.3 = (bf16[2,8,192,256]{3,2,1,0:T(8,128)(2,1)}, bf16[8,192,256]{2,1,0:T(8,128)(2,1)}, bf16[2,256,128]{2,1,0:T(8,128)(2,1)}) custom-call(s32[1]{0:T(128)} %bitcast.2.slab, f32[1,2]{1,0:T(1,128)} %weights.3, bf16[2,192,192]{2,1,0:T(8,128)(2,1)} %constant.172.clone.table_y, bf16[512,512]{1,0:T(8,128)(2,1)} %constant.173.clone.table_z, ...), custom_call_target="tpu_custom_call" | custom-call | flops 1409286144 | bytes 3145728 | tf_op jit(solution)/shard_map/make_field/pallas_call | solution.py:418
  138.4 5.5 %go_back.3 = (bf16[24,16,256]{2,1,0:T(8,128)(2,1)}, bf16[24,16,256]{2,1,0:T(8,128)(2,1)}, bf16[24,16,256]{2,1,0:T(8,128)(2,1)}, bf16[24,16,256]{2,1,0:T(8,128)(2...) custom-call(s32[1]{0:T(128)} %bitcast.2.slab, ...), custom_call_target="tpu_custom_call" | custom-call | flops 1409286144 | bytes 3145728 | tf_op jit(solution)/shard_map/go_back/pallas_call | solution.py:578
  150.1 9.8 %go_back.2 = (bf16[24,32,256]{2,1,0:T(8,128)(2,1)}, bf16[24,32,256]{2,1,0:T(8,128)(2,1)}, bf16[24,32,256]{2,1,0:T(8,128)(2,1)}, bf16[24,32,256]{2,1,0:T(8,128)(2...) custom-call(s32[1]{0:T(128)} %bitcast.2.slab, ...), custom_call_target="tpu_custom_call" | custom-call | flops 2818572288 | bytes 6291456 | tf_op jit(solution)/shard_map/go_back/pallas_call | solution.py:578
  160.0 3.4 %collective-permute-start.25 = (bf16[24,32,256]{2,1,0:T(8,128)(2,1)}, bf16[24,32,256]{2,1,0:T(8,128)(2,1)S(1)}, u32[]{:S(2)}, u32[]{:S(2)}) collective-permute-start(bf16[24,32,256]{2,1,0:T(8,128)(2,1)} %get-tuple-element.202), channel_id=1, source_target_pairs={{0,4},{1,5},{2,6},{3,7},{4,0},{5,1},{6,2},{7,3},{8,12},{9,13},{10,... | collective-permute-start | bytes 1179656 | tf_op jit(solution)/shard_map/ppermute | solution.py:799
  164.3 8.7 %collective-permute-done.19.refs_10_ = bf16[24,16,256]{2,1,0:T(8,128)(2,1)S(1)} collective-permute-done((bf16[24,16,256]{2,1,0:T(8,128)(2,1)}, bf16[24,16,256]{2,1,0:T(8,128)(2,1)S(1)}, u32[]{:S(2)}, u32[]{:S(2)}) %collective-permute-start.19) | collective-permute-done | bytes 196640 | tf_op jit(solution)/shard_map/ppermute | solution.py:799
  173.0 8.2 %collective-permute-start.22 = (bf16[24,16,256]{2,1,0:T(8,128)(2,1)S(1)}, bf16[24,16,256]{2,1,0:T(8,128)(2,1)S(1)}, u32[]{:S(2)}, u32[]{:S(2)}) collective-permute-start(bf16[24,16,256]{2,1,0:T(8,128)(2,1)S(1)} %copy-done.30), channel_id=1, source_target_pairs={{0,6},{1,7},{2,0},{3,1},{4,2},{5,3},{6,4},{7,5},{8,14},{9,15},{10,... | collective-permute-start | bytes 589832 | tf_op jit(solution)/shard_map/ppermute | solution.py:799
  182.6 8.5 %collective-permute-start.24 = (bf16[24,16,256]{2,1,0:T(8,128)(2,1)S(1)}, bf16[24,16,256]{2,1,0:T(8,128)(2,1)S(1)}, u32[]{:S(2)}, u32[]{:S(2)}) collective-permute-start(bf16[24,16,256]{2,1,0:T(8,128)(2,1)S(1)} %copy-done.27), channel_id=1, source_target_pairs={{0,7},{1,0},{2,1},{3,2},{4,3},{5,4},{6,5},{7,6},{8,15},{9,8},{10,9... | collective-permute-start | bytes 589832 | tf_op jit(solution)/shard_map/ppermute | solution.py:799
  193.5 27.4 %collective-permute-done.22.refs_13_ = bf16[24,16,256]{2,1,0:T(8,128)(2,1)S(1)} collective-permute-done((bf16[24,16,256]{2,1,0:T(8,128)(2,1)S(1)}, bf16[24,16,256]{2,1,0:T(8,128)(2,1)S(1)}, u32[]{:S(2)}, u32[]{:S(2)}) %collective-permute-start.22) | collective-permute-done | bytes 196640 | tf_op jit(solution)/shard_map/ppermute | solution.py:799
  231.0 6.3 %collective-permute-done.27.refs_3_ = bf16[24,32,256]{2,1,0:T(8,128)(2,1)S(1)} collective-permute-done((bf16[24,32,256]{2,1,0:T(8,128)(2,1)}, bf16[24,32,256]{2,1,0:T(8,128)(2,1)S(1)}, u32[]{:S(2)}, u32[]{:S(2)}) %collective-permute-start.27) | collective-permute-done | bytes 393248 | tf_op jit(solution)/shard_map/ppermute | solution.py:799
  237.3 7.0 %collective-permute-done.29.refs_5_ = bf16[24,32,256]{2,1,0:T(8,128)(2,1)S(1)} collective-permute-done((bf16[24,32,256]{2,1,0:T(8,128)(2,1)}, bf16[24,32,256]{2,1,0:T(8,128)(2,1)S(1)}, u32[]{:S(2)}, u32[]{:S(2)}) %collective-permute-start.29) | collective-permute-done | bytes 393248 | tf_op jit(solution)/shard_map/ppermute | solution.py:799
  244.3 4.7 %collective-permute-done.31.refs_7_ = bf16[24,32,256]{2,1,0:T(8,128)(2,1)} collective-permute-done((bf16[24,32,256]{2,1,0:T(8,128)(2,1)}, bf16[24,32,256]{2,1,0:T(8,128)(2,1)}, u32[]{:S(2)}, u32[]{:S(2)}) %collective-permute-start.31) | collective-permute-done | bytes 393248 | tf_op jit(solution)/shard_map/ppermute | solution.py:799
  248.9 8.9 %last_x.1 = bf16[2,192,24,256]{3,2,1,0:T(8,128)(2,1)} custom-call(f32[192]{0:T(256)} %constant.177.clone.frequency_x, f32[24,256]{1,0:T(8,128)} %broadcast_add_fusion.frequency_yz, bf16[384,384]{1,0:T(8,128)(2,1)} %dynamic-slice_bitcast_fusion.table, bf16[2,192,24,256]{3,2,1,0:T(8,128)(2,1)} %bitcast.20, bf16[24,32,256]{2,1,0:T(8,128)(2,1)} %get-tuple-element.201.refs_0_, ...), custom_call_target="tpu_custom_call" | custom-call | flops 1811939328 | bytes 14155776 | tf_op jit(solution)/shard_map/last_x/pallas_call | solution.py:636
  (161 shorter events, 51.9 us)
Async XLA Ops:
  7.2 152.8 %all-reduce.3.cloned.1.call-start = ((), (), s32[]{:S(2)}) async-start(), calls=%async_computation | async-start | bytes 3145728 | tf_op jit(solution)/shard_map/psum | solution.py:779
  14.1 27.9 %collective-permute-start.3 = (bf16[24,32,256]{2,1,0:T(8,128)(2,1)}, bf16[24,32,256]{2,1,0:T(8,128)(2,1)S(1)}, u32[]{:S(2)}, u32[]{:S(2)}) collective-permute-start(bf16[24,32,256]{2,1,0:T(8,128)(2,1)} %get-tuple-element.142), channel_id=1, source_target_pairs={{0,4},{1,5},{2,6},{3,7},{4,0},{5,1},{6,2},{7,3},{8,12},{9,13},{10,... | collective-permute-start | bytes 1179656 | tf_op jit(solution)/shard_map/ppermute | solution.py:762
  16.7 34.9 %collective-permute-start.4 = (bf16[24,32,256]{2,1,0:T(8,128)(2,1)}, bf16[24,32,256]{2,1,0:T(8,128)(2,1)S(1)}, u32[]{:S(2)}, u32[]{:S(2)}) collective-permute-start(bf16[24,32,256]{2,1,0:T(8,128)(2,1)} %get-tuple-element.145), channel_id=1, source_target_pairs={{0,5},{1,4},{2,7},{3,6},{4,1},{5,0},{6,3},{7,2},{8,13},{9,12},{10,... | collective-permute-start | bytes 1179656 | tf_op jit(solution)/shard_map/ppermute | solution.py:762
  18.0 44.9 %collective-permute-start.1 = (bf16[24,32,256]{2,1,0:T(8,128)(2,1)}, bf16[24,32,256]{2,1,0:T(8,128)(2,1)S(1)}, u32[]{:S(2)}, u32[]{:S(2)}) collective-permute-start(bf16[24,32,256]{2,1,0:T(8,128)(2,1)} %get-tuple-element.136), channel_id=1, source_target_pairs={{0,2},{1,3},{2,0},{3,1},{4,6},{5,7},{6,4},{7,5},{8,10},{9,11},{10,... | collective-permute-start | bytes 1179656 | tf_op jit(solution)/shard_map/ppermute | solution.py:762
  24.7 38.7 %collective-permute-start.2 = (bf16[24,32,256]{2,1,0:T(8,128)(2,1)}, bf16[24,32,256]{2,1,0:T(8,128)(2,1)S(1)}, u32[]{:S(2)}, u32[]{:S(2)}) collective-permute-start(bf16[24,32,256]{2,1,0:T(8,128)(2,1)} %get-tuple-element.139), channel_id=1, source_target_pairs={{0,3},{1,2},{2,1},{3,0},{4,7},{5,6},{6,5},{7,4},{8,11},{9,10},{10,... | collective-permute-start | bytes 1179656 | tf_op jit(solution)/shard_map/ppermute | solution.py:762
  42.0 34.5 %collective-permute-start.5 = (bf16[24,32,256]{2,1,0:T(8,128)(2,1)}, bf16[24,32,256]{2,1,0:T(8,128)(2,1)S(1)}, u32[]{:S(2)}, u32[]{:S(2)}) collective-permute-start(bf16[24,32,256]{2,1,0:T(8,128)(2,1)} %get-tuple-element.148), channel_id=1, source_target_pairs={{0,6},{1,7},{2,4},{3,5},{4,2},{5,3},{6,0},{7,1},{8,14},{9,15},{10,... | collective-permute-start | bytes 1179656 | tf_op jit(solution)/shard_map/ppermute | solution.py:762
  51.7 33.1 %collective-permute-start.6 = (bf16[24,32,256]{2,1,0:T(8,128)(2,1)}, bf16[24,32,256]{2,1,0:T(8,128)(2,1)S(1)}, u32[]{:S(2)}, u32[]{:S(2)}) collective-permute-start(bf16[24,32,256]{2,1,0:T(8,128)(2,1)} %get-tuple-element.151), channel_id=1, source_target_pairs={{0,7},{1,6},{2,5},{3,4},{4,3},{5,2},{6,1},{7,0},{8,15},{9,14},{10,... | collective-permute-start | bytes 1179656 | tf_op jit(solution)/shard_map/ppermute | solution.py:762
  62.9 36.8 %collective-permute-start.7 = (bf16[24,16,256]{2,1,0:T(8,128)(2,1)}, bf16[24,16,256]{2,1,0:T(8,128)(2,1)S(1)}, u32[]{:S(2)}, u32[]{:S(2)}) collective-permute-start(bf16[24,16,256]{2,1,0:T(8,128)(2,1)} %get-tuple-element.161), channel_id=1, source_target_pairs={{0,1},{1,0},{2,3},{3,2},{4,5},{5,4},{6,7},{7,6},{8,9},{9,8},{10,11... | collective-permute-start | bytes 589832 | tf_op jit(solution)/shard_map/ppermute | solution.py:762
  84.8 20.3 %collective-permute-start.10 = (bf16[24,16,256]{2,1,0:T(8,128)(2,1)}, bf16[24,16,256]{2,1,0:T(8,128)(2,1)S(1)}, u32[]{:S(2)}, u32[]{:S(2)}) collective-permute-start(bf16[24,16,256]{2,1,0:T(8,128)(2,1)} %get-tuple-element.166), channel_id=1, source_target_pairs={{0,4},{1,5},{2,6},{3,7},{4,0},{5,1},{6,2},{7,3},{8,12},{9,13},{10,... | collective-permute-start | bytes 589832 | tf_op jit(solution)/shard_map/ppermute | solution.py:762
  98.0 130.1 %all-reduce.5.cloned.1.call-start = ((), (), s32[]{:S(2)}) async-start(), calls=%async_computation.1 | async-start | bytes 1572864 | tf_op jit(solution)/shard_map/psum | solution.py:809
  105.7 20.3 %collective-permute-start.12 = (bf16[24,16,256]{2,1,0:T(8,128)(2,1)S(1)}, bf16[24,16,256]{2,1,0:T(8,128)(2,1)S(1)}, u32[]{:S(2)}, u32[]{:S(2)}) collective-permute-start(bf16[24,16,256]{2,1,0:T(8,128)(2,1)S(1)} %copy-done.24), channel_id=1, source_target_pairs={{0,6},{1,7},{2,4},{3,5},{4,2},{5,3},{6,0},{7,1},{8,14},{9,15},{10,... | collective-permute-start | bytes 589832 | tf_op jit(solution)/shard_map/ppermute | solution.py:762
  106.0 26.4 %collective-permute-start.14 = (bf16[2,256,128]{2,1,0:T(8,128)(2,1)}, bf16[2,256,128]{2,1,0:T(8,128)(2,1)S(1)}, u32[]{:S(2)}, u32[]{:S(2)}) collective-permute-start(bf16[2,256,128]{2,1,0:T(8,128)(2,1)} %get-tuple-element.174), channel_id=1, source_target_pairs={{1,0},{2,1},{3,2},{4,3},{5,4},{6,5},{7,6},{0,7},{9,8},{10,9},{11,1... | collective-permute-start | bytes 393224 | tf_op jit(solution)/shard_map/ppermute | solution.py:777
  109.5 23.0 %collective-permute-start.15 = (bf16[2,256,128]{2,1,0:T(8,128)(2,1)}, bf16[2,256,128]{2,1,0:T(8,128)(2,1)S(1)}, u32[]{:S(2)}, u32[]{:S(2)}) collective-permute-start(bf16[2,256,128]{2,1,0:T(8,128)(2,1)} %get-tuple-element.175), channel_id=1, source_target_pairs={{0,1},{1,2},{2,3},{3,4},{4,5},{5,6},{6,7},{7,0},{8,9},{9,10},{10,1... | collective-permute-start | bytes 393224 | tf_op jit(solution)/shard_map/ppermute | solution.py:778
  143.9 29.1 %collective-permute-start.19 = (bf16[24,16,256]{2,1,0:T(8,128)(2,1)}, bf16[24,16,256]{2,1,0:T(8,128)(2,1)S(1)}, u32[]{:S(2)}, u32[]{:S(2)}) collective-permute-start(bf16[24,16,256]{2,1,0:T(8,128)(2,1)} %get-tuple-element.194), channel_id=1, source_target_pairs={{0,3},{1,4},{2,5},{3,6},{4,7},{5,0},{6,1},{7,2},{8,11},{9,12},{10,... | collective-permute-start | bytes 589832 | tf_op jit(solution)/shard_map/ppermute | solution.py:799
  146.0 35.2 %collective-permute-start.20 = (bf16[24,16,256]{2,1,0:T(8,128)(2,1)}, bf16[24,16,256]{2,1,0:T(8,128)(2,1)S(1)}, u32[]{:S(2)}, u32[]{:S(2)}) collective-permute-start(bf16[24,16,256]{2,1,0:T(8,128)(2,1)} %get-tuple-element.195), channel_id=1, source_target_pairs={{0,5},{1,6},{2,7},{3,0},{4,1},{5,2},{6,3},{7,4},{8,13},{9,14},{10,... | collective-permute-start | bytes 589832 | tf_op jit(solution)/shard_map/ppermute | solution.py:799
  146.9 35.7 %collective-permute-start.21 = (bf16[24,16,256]{2,1,0:T(8,128)(2,1)}, bf16[24,16,256]{2,1,0:T(8,128)(2,1)S(1)}, u32[]{:S(2)}, u32[]{:S(2)}) collective-permute-start(bf16[24,16,256]{2,1,0:T(8,128)(2,1)} %get-tuple-element.196), channel_id=1, source_target_pairs={{0,2},{1,3},{2,4},{3,5},{4,6},{5,7},{6,0},{7,1},{8,10},{9,11},{10,... | collective-permute-start | bytes 589832 | tf_op jit(solution)/shard_map/ppermute | solution.py:799
  160.0 63.1 %collective-permute-start.25 = (bf16[24,32,256]{2,1,0:T(8,128)(2,1)}, bf16[24,32,256]{2,1,0:T(8,128)(2,1)S(1)}, u32[]{:S(2)}, u32[]{:S(2)}) collective-permute-start(bf16[24,32,256]{2,1,0:T(8,128)(2,1)} %get-tuple-element.202), channel_id=1, source_target_pairs={{0,4},{1,5},{2,6},{3,7},{4,0},{5,1},{6,2},{7,3},{8,12},{9,13},{10,... | collective-permute-start | bytes 1179656 | tf_op jit(solution)/shard_map/ppermute | solution.py:799
  163.4 62.1 %collective-permute-start.26 = (bf16[24,32,256]{2,1,0:T(8,128)(2,1)}, bf16[24,32,256]{2,1,0:T(8,128)(2,1)S(1)}, u32[]{:S(2)}, u32[]{:S(2)}) collective-permute-start(bf16[24,32,256]{2,1,0:T(8,128)(2,1)} %get-tuple-element.203), channel_id=1, source_target_pairs={{0,3},{1,4},{2,5},{3,6},{4,7},{5,0},{6,1},{7,2},{8,11},{9,12},{10,... | collective-permute-start | bytes 1179656 | tf_op jit(solution)/shard_map/ppermute | solution.py:799
  173.0 48.0 %collective-permute-start.22 = (bf16[24,16,256]{2,1,0:T(8,128)(2,1)S(1)}, bf16[24,16,256]{2,1,0:T(8,128)(2,1)S(1)}, u32[]{:S(2)}, u32[]{:S(2)}) collective-permute-start(bf16[24,16,256]{2,1,0:T(8,128)(2,1)S(1)} %copy-done.30), channel_id=1, source_target_pairs={{0,6},{1,7},{2,0},{3,1},{4,2},{5,3},{6,4},{7,5},{8,14},{9,15},{10,... | collective-permute-start | bytes 589832 | tf_op jit(solution)/shard_map/ppermute | solution.py:799
  181.2 39.7 %collective-permute-start.23 = (bf16[24,16,256]{2,1,0:T(8,128)(2,1)S(1)}, bf16[24,16,256]{2,1,0:T(8,128)(2,1)S(1)}, u32[]{:S(2)}, u32[]{:S(2)}) collective-permute-start(bf16[24,16,256]{2,1,0:T(8,128)(2,1)S(1)} %copy-done.29), channel_id=1, source_target_pairs={{0,1},{1,2},{2,3},{3,4},{4,5},{5,6},{6,7},{7,0},{8,9},{9,10},{10,1... | collective-permute-start | bytes 589832 | tf_op jit(solution)/shard_map/ppermute | solution.py:799
  182.6 38.4 %collective-permute-start.24 = (bf16[24,16,256]{2,1,0:T(8,128)(2,1)S(1)}, bf16[24,16,256]{2,1,0:T(8,128)(2,1)S(1)}, u32[]{:S(2)}, u32[]{:S(2)}) collective-permute-start(bf16[24,16,256]{2,1,0:T(8,128)(2,1)S(1)} %copy-done.27), channel_id=1, source_target_pairs={{0,7},{1,0},{2,1},{3,2},{4,3},{5,4},{6,5},{7,6},{8,15},{9,8},{10,9... | collective-permute-start | bytes 589832 | tf_op jit(solution)/shard_map/ppermute | solution.py:799
  221.1 23.2 %collective-permute-start.29 = (bf16[24,32,256]{2,1,0:T(8,128)(2,1)}, bf16[24,32,256]{2,1,0:T(8,128)(2,1)S(1)}, u32[]{:S(2)}, u32[]{:S(2)}) collective-permute-start(bf16[24,32,256]{2,1,0:T(8,128)(2,1)} %get-tuple-element.206), channel_id=1, source_target_pairs={{0,6},{1,7},{2,0},{3,1},{4,2},{5,3},{6,4},{7,5},{8,14},{9,15},{10,... | collective-permute-start | bytes 1179656 | tf_op jit(solution)/shard_map/ppermute | solution.py:799
  223.1 21.2 %collective-permute-start.30 = (bf16[24,32,256]{2,1,0:T(8,128)(2,1)}, bf16[24,32,256]{2,1,0:T(8,128)(2,1)}, u32[]{:S(2)}, u32[]{:S(2)}) collective-permute-start(bf16[24,32,256]{2,1,0:T(8,128)(2,1)} %get-tuple-element.207), channel_id=1, source_target_pairs={{0,1},{1,2},{2,3},{3,4},{4,5},{5,6},{6,7},{7,0},{8,9},{9,10},{10,1... | collective-permute-start | bytes 1179656 | tf_op jit(solution)/shard_map/ppermute | solution.py:799
  225.5 23.4 %collective-permute-start.31 = (bf16[24,32,256]{2,1,0:T(8,128)(2,1)}, bf16[24,32,256]{2,1,0:T(8,128)(2,1)}, u32[]{:S(2)}, u32[]{:S(2)}) collective-permute-start(bf16[24,32,256]{2,1,0:T(8,128)(2,1)} %get-tuple-element.208), channel_id=1, source_target_pairs={{0,7},{1,0},{2,1},{3,2},{4,3},{5,4},{6,5},{7,6},{8,15},{9,8},{10,9... | collective-permute-start | bytes 1179656 | tf_op jit(solution)/shard_map/ppermute | solution.py:799
  (49 other events, 872.0 us)
Sparse Core Ops, SparseCore 0:
  98.2 43.7 all-reduce.2
  193.0 35.1 all-reduce.4
